TPU v7x, 1024 devices: a whole 4x8x16 slice. The times are simulated.
1024 devices in a mesh: gx: 16 (over y, x_lo), gy: 4 (over x_hi, core), gz: 16 (over z).
Axes of the slice: x: 4 (x_hi: 2, x_lo: 2; x = x_hi * 2 + x_lo), y: 8, z: 16, core: 2. Of those that a mesh axis runs over, the one named last changes fastest.
Arguments:
- counts: int32 [64, 32, 2048], P('gx', 'gy', 'gz'), may hold values from 0 to 4, as said below
- offsets: float32 [3, 4, 64, 32, 2048], P(None, None, 'gx', 'gy', 'gz'), may hold values from 0 to 1
- volume: float32 [4, 64, 32, 2048], P(None, 'gx', 'gy', 'gz'), may hold values from 0.02 to 0.25
- beta: float32 [4, 64, 32, 2048], P(None, 'gx', 'gy', 'gz'), may hold values from 0.3 to 3
- particle_velocity: float32 [3, 4, 64, 32, 2048], P(None, None, 'gx', 'gy', 'gz'), may hold values from -6 to 6
- gas_velocity: float32 [3, 64, 32, 2048], P(None, 'gx', 'gy', 'gz'), may hold values from -6 to 6
Outputs:
- filtered: float32 [5, 64, 32, 2048], P(None, 'gx', 'gy', 'gz')
- drag_force: float32 [3, 4, 64, 32, 2048], P(None, None, 'gx', 'gy', 'gz')
Inputs may be any that keep to these rules, and one draw needn't show every extreme that they name: `counts`: every cell of the bottom layer holds 4 particles; cells in the lower half of the bed hold up to 4, cells in the upper half up to 2. Slots at or above a cell's count carry no particle.
All inputs are finite; a program needn't handle non-finite values.
Results may differ from a plain program's by a relative error of at most 0.00002.
Values sent between devices are 32-bit elements; how exact they have to be, the bound alone decides.
A program may use at most 128 MiB of HBM per device.

v0:
```python
import jax
import jax.numpy as jnp
from jax import lax
from jax.sharding import PartitionSpec as P

ITERS = 4


SIGMA = 0.6
FILTER = 2.0


def padded_2(block, sides, width):
    for axis, dim in sides:
        count = lax.axis_size(axis)
        forward = [(i, i + 1) for i in range(count - 1)]
        backward = [(target, source) for source, target in forward]
        low = lax.ppermute(
            lax.slice_in_dim(block, block.shape[dim] - width, None, axis=dim), axis, forward
        )
        high = lax.ppermute(lax.slice_in_dim(block, 0, width, axis=dim), axis, backward)
        block = jnp.concatenate([low, block, high], axis=dim)
    return block


def kernel_weights(offset):
    curves = [
        jnp.exp(-jnp.square(stride + 0.5 - offset) / (2.0 * SIGMA * SIGMA))
        for stride in (-1.0, 0.0, 1.0)
    ]
    weight_sum = curves[0] + curves[1] + curves[2]
    return [single / weight_sum for single in curves]


def window_of(first_x, first_y, first_z, size_x, size_y, size_z):
    return (
        slice(first_x, first_x + size_x),
        slice(first_y, first_y + size_y),
        slice(first_z, first_z + size_z),
    )


def neighbour_sum(padded):
    return (
        padded[:, 2:, 1:-1, 1:-1]
        + padded[:, :-2, 1:-1, 1:-1]
        + padded[:, 1:-1, 2:, 1:-1]
        + padded[:, 1:-1, :-2, 1:-1]
        + padded[:, 1:-1, 1:-1, 2:]
        + padded[:, 1:-1, 1:-1, :-2]
    )


def deposit_owner(sources, offsets):
    size_x, size_y, size_z = sources.shape[2:]
    stacked = jnp.concatenate([sources, offsets], axis=0)
    extended = padded_2(stacked, (("gx", 2), ("gy", 3), ("gz", 4)), 1)
    padded_sources = extended[:5]
    weight_x = kernel_weights(extended[5])
    weight_y = kernel_weights(extended[6])
    weight_z = kernel_weights(extended[7])
    deposited = jnp.zeros((5, size_x, size_y, size_z), jnp.float32)
    for index_x in range(3):
        for index_y in range(3):
            for index_z in range(3):
                window = window_of(2 - index_x, 2 - index_y, 2 - index_z, size_x, size_y, size_z)
                factor = (
                    weight_x[index_x][(slice(None),) + window]
                    * weight_y[index_y][(slice(None),) + window]
                    * weight_z[index_z][(slice(None),) + window]
                )
                deposited = deposited + jnp.sum(
                    padded_sources[(slice(None), slice(None)) + window] * factor[None], axis=1
                )
    return deposited


def interpolate(gas_padded, offsets, beta, particle_velocity, occupied):
    size_x, size_y, size_z = beta.shape[1:]
    weight_x = kernel_weights(offsets[0])
    weight_y = kernel_weights(offsets[1])
    weight_z = kernel_weights(offsets[2])
    gas_at = jnp.zeros(particle_velocity.shape, jnp.float32)
    for index_x in range(3):
        for index_y in range(3):
            for index_z in range(3):
                window = window_of(index_x, index_y, index_z, size_x, size_y, size_z)
                factor = weight_x[index_x] * weight_y[index_y] * weight_z[index_z]
                gas_at = gas_at + gas_padded[(slice(None),) + window][:, None] * factor[None]
    return occupied[None] * beta[None] * (gas_at - particle_velocity)


def shards(counts, offsets, volume, beta, particle_velocity, gas_velocity):
    slot_count = offsets.shape[1]
    slot_iota = lax.broadcasted_iota(jnp.int32, (slot_count,) + counts.shape, 0)
    occupied = (slot_iota < counts[None]).astype(jnp.float32)
    sources = (
        jnp.stack(
            [
                volume,
                beta,
                beta * particle_velocity[0],
                beta * particle_velocity[1],
                beta * particle_velocity[2],
            ]
        )
        * occupied[None]
    )
    deposited = deposit_owner(sources, offsets)
    current = deposited
    for sweep_index in range(ITERS):
        outgoing = current
        padded = padded_2(outgoing, (("gx", 1), ("gy", 2), ("gz", 3)), 1)
        current = (deposited + FILTER * neighbour_sum(padded)) / (1.0 + 6.0 * FILTER)
    gas_padded = padded_2(gas_velocity, (("gx", 1), ("gy", 2), ("gz", 3)), 1)
    drag_force = interpolate(gas_padded, offsets, beta, particle_velocity, occupied)
    return (current, drag_force)


def solution(mesh):
    in_specs = (
        P("gx", "gy", "gz"),
        P(None, None, "gx", "gy", "gz"),
        P(None, "gx", "gy", "gz"),
        P(None, "gx", "gy", "gz"),
        P(None, None, "gx", "gy", "gz"),
        P(None, "gx", "gy", "gz"),
    )
    out_specs = (P(None, "gx", "gy", "gz"), P(None, None, "gx", "gy", "gz"))
    return jax.shard_map(shards, mesh=mesh, in_specs=in_specs, out_specs=out_specs, check_vma=False)
```

profile of v0, /device:TPU:473, one launch (start us, length us, event | category | flops | bytes accessed | tf_op | source)
XLA Modules:
  0.0 207.1 jit_solution(10024047506512664216)
XLA Ops:
  2.0 3.0 %collective-permute-start.31 = (f32[3,1,8,128]{3,2,1,0:T(8,128)}, f32[3,1,8,128]{3,2,1,0:T(8,128)S(1)}, u32[]{:S(2)}, u32[]{:S(2)}) collective-permute-start(f32[3,1,8,128]{3,2,1,0:T(8,128)} %get-tuple-element.174), channel_id=1, source_target_pairs={{64,0},{128,64},{192,128},{256,192},{320,256},{384,320},{448,384},... | collective-permute-start | bytes 36872 | tf_op jit(solution)/shard_map/ppermute | solution.py:21
  5.0 2.3 %collective-permute-start.30 = (f32[3,1,8,128]{3,2,1,0:T(8,128)}, f32[3,1,8,128]{3,2,1,0:T(8,128)}, u32[]{:S(2)}, u32[]{:S(2)}) collective-permute-start(f32[3,1,8,128]{3,2,1,0:T(8,128)} %get-tuple-element.175), channel_id=1, source_target_pairs={{0,64},{64,128},{128,192},{192,256},{256,320},{320,384},{384,448},... | collective-permute-start | bytes 36872 | tf_op jit(solution)/shard_map/ppermute | solution.py:18
  14.7 5.2 %collective-permute-start = (f32[8,4,1,8,128]{4,1,3,2,0:T(4,128)S(1)}, f32[8,4,1,8,128]{4,1,3,2,0:T(4,128)S(1)}, u32[]{:S(2)}, u32[]{:S(2)}) collective-permute-start(f32[8,4,1,8,128]{4,1,3,2,0:T(4,128)S(1)} %get-tuple-element.55), channel_id=1, source_target_pairs={{0,64},{64,128},{128,192},{192,256},{256,320},{320,384},{384,448},... | collective-permute-start | bytes 393224 | tf_op jit(solution)/shard_map/ppermute | solution.py:18
  20.0 1.9 collective-permute-start.1
  25.7 6.9 %collective-permute-start.2 = (f32[8,4,6,1,128]{4,1,3,2,0:T(4,128)S(1)}, f32[8,4,6,1,128]{4,1,3,2,0:T(4,128)S(1)}, u32[]{:S(2)}, u32[]{:S(2)}) collective-permute-start(f32[8,4,6,1,128]{4,1,3,2,0:T(4,128)S(1)} %get-tuple-element.53), channel_id=1, source_target_pairs={{0,16},{16,32},{32,48},{1,17},{17,33},{33,49},{2,18},{18,34},{34,5... | collective-permute-start | bytes 294920 | tf_op jit(solution)/shard_map/ppermute | solution.py:18
  32.7 1.9 collective-permute-start.3
  35.5 4.6 %collective-permute-done.3 = f32[8,4,6,1,128]{4,1,3,2,0:T(4,128)S(1)} collective-permute-done((f32[8,4,6,1,128]{4,1,3,2,0:T(4,128)S(1)}, f32[8,4,6,1,128]{4,1,3,2,0:T(4,128)S(1)}, u32[]{:S(2)}, u32[]{:S(2)}) %collective-permute-start.3) | collective-permute-done | bytes 98336 | tf_op jit(solution)/shard_map/ppermute | solution.py:21
  40.9 1.9 copy.34
  44.0 5.2 %collective-permute-start.5 = (f32[8,4,6,10,1]{3,0,4,2,1:T(8,128)S(1)}, f32[8,4,6,10,1]{3,0,4,2,1:T(8,128)}, u32[]{:S(2)}, u32[]{:S(2)}) collective-permute-start(f32[8,4,6,10,1]{3,0,4,2,1:T(8,128)S(1)} %copy.36), channel_id=1, source_target_pairs={{0,1},{1,2},{2,3},{3,4},{4,5},{5,6},{6,7},{7,8},{8,9},{9,10},{10,1... | collective-permute-start | bytes 23048 | tf_op jit(solution)/shard_map/ppermute | solution.py:18
  49.2 2.1 %collective-permute-start.4 = (f32[8,4,6,10,1]{3,0,4,2,1:T(8,128)}, f32[8,4,6,10,1]{3,0,4,2,1:T(8,128)S(1)}, u32[]{:S(2)}, u32[]{:S(2)}) collective-permute-start(f32[8,4,6,10,1]{3,0,4,2,1:T(8,128)} %copy.34), channel_id=1, source_target_pairs={{1,0},{2,1},{3,2},{4,3},{5,4},{6,5},{7,6},{8,7},{9,8},{10,9},{11,1... | collective-permute-start | bytes 23048 | tf_op jit(solution)/shard_map/ppermute | solution.py:21
  52.8 3.2 %collective-permute-done.4 = f32[8,4,6,10,1]{3,0,4,2,1:T(8,128)S(1)} collective-permute-done((f32[8,4,6,10,1]{3,0,4,2,1:T(8,128)}, f32[8,4,6,10,1]{3,0,4,2,1:T(8,128)S(1)}, u32[]{:S(2)}, u32[]{:S(2)}) %collective-permute-start.4) | collective-permute-done | bytes 7712 | tf_op jit(solution)/shard_map/ppermute | solution.py:21
  57.3 2.1 %copy.37 = f32[8,4,6,10,1]{4,1,3,2,0:T(4,128)S(1)} copy(f32[8,4,6,10,1]{3,0,4,2,1:T(8,128)} %collective-permute-done.5) | data formatting | bytes 15360 | tf_op jit(solution)/shard_map/ppermute | solution.py:18
  59.4 3.6 %pad_maximum_fusion.1 = f32[8,4,6,10,130]{4,1,3,2,0:T(4,128)S(1)} fusion(f32[8,4,6,10,1]{4,1,3,2,0:T(4,128)S(1)} %copy.35, f32[8,4,6,1,128]{4,1,3,2,0:T(4,128)S(1)} %collective-permute-done.3, f32[8,4,1,8,128]{4,1,3,2,0:T(4,128)S(1)} %collective-permute-done.1, f32[3,4,4,8,128]{4,1,3,2,0:T(4,128)S(1)} %copy.33, f32[5,4,4,8,128]{4,1,3,2,0:T(4,128)S(1)} %bitcast.143, ...), kind=kLoop, calls=%fused_computation.1 | loop fusion | flops 1747200 | bytes 1996800 | tf_op jit(solution)/shard_map/concatenate | solution.py:22
  68.5 4.2 %pad_maximum_fusion = (f32[8,4,6,10,129]{4,1,3,2,0:T(4,128)S(1)}, f32[8,4,6,10,129]{4,1,3,2,0:T(4,128)S(1)}) fusion(f32[8,4,6,10,1]{4,1,3,2,0:T(4,128)S(1)} %copy.35, f32[8,4,6,1,128]{4,1,3,2,0:T(4,128)S(1)} %collective-permute-done.3, f32[8,4,1,8,128]{4,1,3,2,0:T(4,128)S(1)} %collective-permute-done.1, f32[3,4,4,8,128]{4,1,3,2,0:T(4,128)S(1)} %copy.33, ...), kind=kLoop, calls=%fused_computation | loop fusion | flops 2972160 | bytes 2979840 | tf_op jit(solution)/shard_map/concatenate | solution.py:22
  72.7 2.0 fusion.27
  74.7 1.8 fusion.25
  77.5 4.1 %collective-permute-start.7 = (f32[5,1,8,128]{3,2,1,0:T(8,128)S(1)}, f32[5,1,8,128]{3,2,1,0:T(8,128)S(1)}, u32[]{:S(2)}, u32[]{:S(2)}) collective-permute-start(f32[5,1,8,128]{3,2,1,0:T(8,128)S(1)} %get-tuple-element.164), channel_id=1, source_target_pairs={{0,64},{64,128},{128,192},{192,256},{256,320},{320,384},{384,448},... | collective-permute-start | bytes 61448 | tf_op jit(solution)/shard_map/ppermute | solution.py:18
  81.6 2.1 %collective-permute-start.6 = (f32[5,1,8,128]{3,2,1,0:T(8,128)S(1)}, f32[5,1,8,128]{3,2,1,0:T(8,128)S(1)}, u32[]{:S(2)}, u32[]{:S(2)}) collective-permute-start(f32[5,1,8,128]{3,2,1,0:T(8,128)S(1)} %get-tuple-element.165), channel_id=1, source_target_pairs={{64,0},{128,64},{192,128},{256,192},{320,256},{384,320},{448,384},... | collective-permute-start | bytes 61448 | tf_op jit(solution)/shard_map/ppermute | solution.py:21
  83.8 2.2 %collective-permute-done.6 = f32[5,1,8,128]{3,2,1,0:T(8,128)S(1)} collective-permute-done((f32[5,1,8,128]{3,2,1,0:T(8,128)S(1)}, f32[5,1,8,128]{3,2,1,0:T(8,128)S(1)}, u32[]{:S(2)}, u32[]{:S(2)}) %collective-permute-start.6) | collective-permute-done | bytes 20512 | tf_op jit(solution)/shard_map/ppermute | solution.py:21
  86.1 5.3 %collective-permute-start.9 = (f32[5,6,1,128]{3,2,1,0:T(1,128)S(1)}, f32[5,6,1,128]{3,2,1,0:T(1,128)S(1)}, u32[]{:S(2)}, u32[]{:S(2)}) collective-permute-start(f32[5,6,1,128]{3,2,1,0:T(1,128)S(1)} %get-tuple-element.148), channel_id=1, source_target_pairs={{0,16},{16,32},{32,48},{1,17},{17,33},{33,49},{2,18},{18,34},{34,5... | collective-permute-start | bytes 46088 | tf_op jit(solution)/shard_map/ppermute | solution.py:18
  91.4 1.9 collective-permute-start.8
  93.4 4.6 %collective-permute-done.8 = f32[5,6,1,128]{3,2,1,0:T(1,128)S(1)} collective-permute-done((f32[5,6,1,128]{3,2,1,0:T(1,128)S(1)}, f32[5,6,1,128]{3,2,1,0:T(1,128)S(1)}, u32[]{:S(2)}, u32[]{:S(2)}) %collective-permute-start.8) | collective-permute-done | bytes 15392 | tf_op jit(solution)/shard_map/ppermute | solution.py:21
  98.1 1.9 collective-permute-start.10
  100.1 4.6 %collective-permute-start.11 = (f32[5,6,10,1]{3,2,1,0:T(8,128)S(1)}, f32[5,6,10,1]{3,2,1,0:T(8,128)S(1)}, u32[]{:S(2)}, u32[]{:S(2)}) collective-permute-start(f32[5,6,10,1]{3,2,1,0:T(8,128)S(1)} %get-tuple-element.109), channel_id=1, source_target_pairs={{0,1},{1,2},{2,3},{3,4},{4,5},{5,6},{6,7},{7,8},{8,9},{9,10},{10,1... | collective-permute-start | bytes 3608 | tf_op jit(solution)/shard_map/ppermute | solution.py:18
  108.0 4.0 %collective-permute-start.13 = (f32[5,1,8,128]{3,2,1,0:T(8,128)S(1)}, f32[5,1,8,128]{3,2,1,0:T(8,128)S(1)}, u32[]{:S(2)}, u32[]{:S(2)}) collective-permute-start(f32[5,1,8,128]{3,2,1,0:T(8,128)S(1)} %get-tuple-element.162), channel_id=1, source_target_pairs={{0,64},{64,128},{128,192},{192,256},{256,320},{320,384},{384,448},... | collective-permute-start | bytes 61448 | tf_op jit(solution)/shard_map/ppermute | solution.py:18
  111.9 2.2 %collective-permute-start.12 = (f32[5,1,8,128]{3,2,1,0:T(8,128)S(1)}, f32[5,1,8,128]{3,2,1,0:T(8,128)S(1)}, u32[]{:S(2)}, u32[]{:S(2)}) collective-permute-start(f32[5,1,8,128]{3,2,1,0:T(8,128)S(1)} %get-tuple-element.163), channel_id=1, source_target_pairs={{64,0},{128,64},{192,128},{256,192},{320,256},{384,320},{448,384},... | collective-permute-start | bytes 61448 | tf_op jit(solution)/shard_map/ppermute | solution.py:21
  116.5 5.1 %collective-permute-start.15 = (f32[5,6,1,128]{3,2,1,0:T(1,128)S(1)}, f32[5,6,1,128]{3,2,1,0:T(1,128)S(1)}, u32[]{:S(2)}, u32[]{:S(2)}) collective-permute-start(f32[5,6,1,128]{3,2,1,0:T(1,128)S(1)} %get-tuple-element.146), channel_id=1, source_target_pairs={{0,16},{16,32},{32,48},{1,17},{17,33},{33,49},{2,18},{18,34},{34,5... | collective-permute-start | bytes 46088 | tf_op jit(solution)/shard_map/ppermute | solution.py:18
  121.6 1.9 collective-permute-start.14
  123.5 4.6 %collective-permute-done.14 = f32[5,6,1,128]{3,2,1,0:T(1,128)S(1)} collective-permute-done((f32[5,6,1,128]{3,2,1,0:T(1,128)S(1)}, f32[5,6,1,128]{3,2,1,0:T(1,128)S(1)}, u32[]{:S(2)}, u32[]{:S(2)}) %collective-permute-start.14) | collective-permute-done | bytes 15392 | tf_op jit(solution)/shard_map/ppermute | solution.py:21
  128.3 1.9 collective-permute-start.16
  130.3 5.3 %collective-permute-start.17 = (f32[5,6,10,1]{3,2,1,0:T(8,128)S(1)}, f32[5,6,10,1]{3,2,1,0:T(8,128)S(1)}, u32[]{:S(2)}, u32[]{:S(2)}) collective-permute-start(f32[5,6,10,1]{3,2,1,0:T(8,128)S(1)} %get-tuple-element.107), channel_id=1, source_target_pairs={{0,1},{1,2},{2,3},{3,4},{4,5},{5,6},{6,7},{7,8},{8,9},{9,10},{10,1... | collective-permute-start | bytes 3608 | tf_op jit(solution)/shard_map/ppermute | solution.py:18
  135.6 2.2 %collective-permute-start.32 = (f32[3,6,1,128]{3,2,1,0:T(1,128)S(1)}, f32[3,6,1,128]{3,2,1,0:T(1,128)S(1)}, u32[]{:S(2)}, u32[]{:S(2)}) collective-permute-start(f32[3,6,1,128]{3,2,1,0:T(1,128)S(1)} %get-tuple-element.169), channel_id=1, source_target_pairs={{0,16},{16,32},{32,48},{1,17},{17,33},{33,49},{2,18},{18,34},{34,5... | collective-permute-start | bytes 27656 | tf_op jit(solution)/shard_map/ppermute | solution.py:18
  137.8 2.1 %collective-permute-start.33 = (f32[3,6,1,128]{3,2,1,0:T(1,128)S(1)}, f32[3,6,1,128]{3,2,1,0:T(1,128)S(1)}, u32[]{:S(2)}, u32[]{:S(2)}) collective-permute-start(f32[3,6,1,128]{3,2,1,0:T(1,128)S(1)} %get-tuple-element.170), channel_id=1, source_target_pairs={{16,0},{32,16},{48,32},{17,1},{33,17},{49,33},{18,2},{34,18},{50,3... | collective-permute-start | bytes 27656 | tf_op jit(solution)/shard_map/ppermute | solution.py:21
  140.2 3.1 %collective-permute-start.19 = (f32[5,1,8,128]{3,2,1,0:T(8,128)S(1)}, f32[5,1,8,128]{3,2,1,0:T(8,128)S(1)}, u32[]{:S(2)}, u32[]{:S(2)}) collective-permute-start(f32[5,1,8,128]{3,2,1,0:T(8,128)S(1)} %get-tuple-element.160), channel_id=1, source_target_pairs={{0,64},{64,128},{128,192},{192,256},{256,320},{320,384},{384,448},... | collective-permute-start | bytes 61448 | tf_op jit(solution)/shard_map/ppermute | solution.py:18
  143.3 3.0 %collective-permute-start.18 = (f32[5,1,8,128]{3,2,1,0:T(8,128)S(1)}, f32[5,1,8,128]{3,2,1,0:T(8,128)S(1)}, u32[]{:S(2)}, u32[]{:S(2)}) collective-permute-start(f32[5,1,8,128]{3,2,1,0:T(8,128)S(1)} %get-tuple-element.161), channel_id=1, source_target_pairs={{64,0},{128,64},{192,128},{256,192},{320,256},{384,320},{448,384},... | collective-permute-start | bytes 61448 | tf_op jit(solution)/shard_map/ppermute | solution.py:21
  148.3 6.6 %collective-permute-start.21 = (f32[5,6,1,128]{3,2,1,0:T(1,128)S(1)}, f32[5,6,1,128]{3,2,1,0:T(1,128)S(1)}, u32[]{:S(2)}, u32[]{:S(2)}) collective-permute-start(f32[5,6,1,128]{3,2,1,0:T(1,128)S(1)} %get-tuple-element.144), channel_id=1, source_target_pairs={{0,16},{16,32},{32,48},{1,17},{17,33},{33,49},{2,18},{18,34},{34,5... | collective-permute-start | bytes 46088 | tf_op jit(solution)/shard_map/ppermute | solution.py:18
  154.9 1.9 collective-permute-start.20
  156.9 3.6 %collective-permute-start.34 = (f32[3,6,10,1]{3,2,1,0:T(8,128)S(1)}, f32[3,6,10,1]{3,2,1,0:T(8,128)S(1)}, u32[]{:S(2)}, u32[]{:S(2)}) collective-permute-start(f32[3,6,10,1]{3,2,1,0:T(8,128)S(1)} %get-tuple-element.140), channel_id=1, source_target_pairs={{0,1},{1,2},{2,3},{3,4},{4,5},{5,6},{6,7},{7,8},{8,9},{9,10},{10,1... | collective-permute-start | bytes 2168 | tf_op jit(solution)/shard_map/ppermute | solution.py:18
  160.6 1.9 collective-permute-start.35
  162.7 1.9 collective-permute-start.22
  164.6 4.6 %collective-permute-start.23 = (f32[5,6,10,1]{3,2,1,0:T(8,128)S(1)}, f32[5,6,10,1]{3,2,1,0:T(8,128)S(1)}, u32[]{:S(2)}, u32[]{:S(2)}) collective-permute-start(f32[5,6,10,1]{3,2,1,0:T(8,128)S(1)} %get-tuple-element.105), channel_id=1, source_target_pairs={{0,1},{1,2},{2,3},{3,4},{4,5},{5,6},{6,7},{7,8},{8,9},{9,10},{10,1... | collective-permute-start | bytes 3608 | tf_op jit(solution)/shard_map/ppermute | solution.py:18
  172.5 3.1 %collective-permute-start.25 = (f32[5,1,8,128]{3,2,1,0:T(8,128)S(1)}, f32[5,1,8,128]{3,2,1,0:T(8,128)S(1)}, u32[]{:S(2)}, u32[]{:S(2)}) collective-permute-start(f32[5,1,8,128]{3,2,1,0:T(8,128)S(1)} %get-tuple-element.158), channel_id=1, source_target_pairs={{0,64},{64,128},{128,192},{192,256},{256,320},{320,384},{384,448},... | collective-permute-start | bytes 61448 | tf_op jit(solution)/shard_map/ppermute | solution.py:18
  175.9 3.2 %collective-permute-start.24 = (f32[5,1,8,128]{3,2,1,0:T(8,128)S(1)}, f32[5,1,8,128]{3,2,1,0:T(8,128)S(1)}, u32[]{:S(2)}, u32[]{:S(2)}) collective-permute-start(f32[5,1,8,128]{3,2,1,0:T(8,128)S(1)} %get-tuple-element.159), channel_id=1, source_target_pairs={{64,0},{128,64},{192,128},{256,192},{320,256},{384,320},{448,384},... | collective-permute-start | bytes 61448 | tf_op jit(solution)/shard_map/ppermute | solution.py:21
  180.6 8.6 %collective-permute-start.27 = (f32[5,6,1,128]{3,2,1,0:T(1,128)S(1)}, f32[5,6,1,128]{3,2,1,0:T(1,128)S(1)}, u32[]{:S(2)}, u32[]{:S(2)}) collective-permute-start(f32[5,6,1,128]{3,2,1,0:T(1,128)S(1)} %get-tuple-element.142), channel_id=1, source_target_pairs={{0,16},{16,32},{32,48},{1,17},{17,33},{33,49},{2,18},{18,34},{34,5... | collective-permute-start | bytes 46088 | tf_op jit(solution)/shard_map/ppermute | solution.py:18
  189.2 1.9 collective-permute-start.26
  191.3 4.4 %collective-permute-done.26 = f32[5,6,1,128]{3,2,1,0:T(1,128)S(1)} collective-permute-done((f32[5,6,1,128]{3,2,1,0:T(1,128)S(1)}, f32[5,6,1,128]{3,2,1,0:T(1,128)S(1)}, u32[]{:S(2)}, u32[]{:S(2)}) %collective-permute-start.26) | collective-permute-done | bytes 15392 | tf_op jit(solution)/shard_map/ppermute | solution.py:21
  195.9 1.9 collective-permute-start.28
  197.8 5.3 %collective-permute-start.29 = (f32[5,6,10,1]{3,2,1,0:T(8,128)S(1)}, f32[5,6,10,1]{3,2,1,0:T(8,128)S(1)}, u32[]{:S(2)}, u32[]{:S(2)}) collective-permute-start(f32[5,6,10,1]{3,2,1,0:T(8,128)S(1)} %get-tuple-element.103), channel_id=1, source_target_pairs={{0,1},{1,2},{2,3},{3,4},{4,5},{5,6},{6,7},{7,8},{8,9},{9,10},{10,1... | collective-permute-start | bytes 3608 | tf_op jit(solution)/shard_map/ppermute | solution.py:18
  (145 shorter events, 42.1 us)
Async XLA Ops:
  2.0 112.2 %collective-permute-start.31 = (f32[3,1,8,128]{3,2,1,0:T(8,128)}, f32[3,1,8,128]{3,2,1,0:T(8,128)S(1)}, u32[]{:S(2)}, u32[]{:S(2)}) collective-permute-start(f32[3,1,8,128]{3,2,1,0:T(8,128)} %get-tuple-element.174), channel_id=1, source_target_pairs={{64,0},{128,64},{192,128},{256,192},{320,256},{384,320},{448,384},... | collective-permute-start | bytes 36872 | tf_op jit(solution)/shard_map/ppermute | solution.py:21
  5.0 99.6 %collective-permute-start.30 = (f32[3,1,8,128]{3,2,1,0:T(8,128)}, f32[3,1,8,128]{3,2,1,0:T(8,128)}, u32[]{:S(2)}, u32[]{:S(2)}) collective-permute-start(f32[3,1,8,128]{3,2,1,0:T(8,128)} %get-tuple-element.175), channel_id=1, source_target_pairs={{0,64},{64,128},{128,192},{192,256},{256,320},{320,384},{384,448},... | collective-permute-start | bytes 36872 | tf_op jit(solution)/shard_map/ppermute | solution.py:18
  14.7 9.2 %collective-permute-start = (f32[8,4,1,8,128]{4,1,3,2,0:T(4,128)S(1)}, f32[8,4,1,8,128]{4,1,3,2,0:T(4,128)S(1)}, u32[]{:S(2)}, u32[]{:S(2)}) collective-permute-start(f32[8,4,1,8,128]{4,1,3,2,0:T(4,128)S(1)} %get-tuple-element.55), channel_id=1, source_target_pairs={{0,64},{64,128},{128,192},{192,256},{256,320},{320,384},{384,448},... | collective-permute-start | bytes 393224 | tf_op jit(solution)/shard_map/ppermute | solution.py:18
  20.0 5.7 %collective-permute-start.1 = (f32[8,4,1,8,128]{4,1,3,2,0:T(4,128)S(1)}, f32[8,4,1,8,128]{4,1,3,2,0:T(4,128)S(1)}, u32[]{:S(2)}, u32[]{:S(2)}) collective-permute-start(f32[8,4,1,8,128]{4,1,3,2,0:T(4,128)S(1)} %get-tuple-element.56), channel_id=1, source_target_pairs={{64,0},{128,64},{192,128},{256,192},{320,256},{384,320},{448,384},... | collective-permute-start | bytes 393224 | tf_op jit(solution)/shard_map/ppermute | solution.py:21
  25.7 9.7 %collective-permute-start.2 = (f32[8,4,6,1,128]{4,1,3,2,0:T(4,128)S(1)}, f32[8,4,6,1,128]{4,1,3,2,0:T(4,128)S(1)}, u32[]{:S(2)}, u32[]{:S(2)}) collective-permute-start(f32[8,4,6,1,128]{4,1,3,2,0:T(4,128)S(1)} %get-tuple-element.53), channel_id=1, source_target_pairs={{0,16},{16,32},{32,48},{1,17},{17,33},{33,49},{2,18},{18,34},{34,5... | collective-permute-start | bytes 294920 | tf_op jit(solution)/shard_map/ppermute | solution.py:18
  32.7 7.4 %collective-permute-start.3 = (f32[8,4,6,1,128]{4,1,3,2,0:T(4,128)S(1)}, f32[8,4,6,1,128]{4,1,3,2,0:T(4,128)S(1)}, u32[]{:S(2)}, u32[]{:S(2)}) collective-permute-start(f32[8,4,6,1,128]{4,1,3,2,0:T(4,128)S(1)} %get-tuple-element.54), channel_id=1, source_target_pairs={{16,0},{32,16},{48,32},{17,1},{33,17},{49,33},{18,2},{34,18},{50,3... | collective-permute-start | bytes 294920 | tf_op jit(solution)/shard_map/ppermute | solution.py:21
  44.0 13.2 %collective-permute-start.5 = (f32[8,4,6,10,1]{3,0,4,2,1:T(8,128)S(1)}, f32[8,4,6,10,1]{3,0,4,2,1:T(8,128)}, u32[]{:S(2)}, u32[]{:S(2)}) collective-permute-start(f32[8,4,6,10,1]{3,0,4,2,1:T(8,128)S(1)} %copy.36), channel_id=1, source_target_pairs={{0,1},{1,2},{2,3},{3,4},{4,5},{5,6},{6,7},{7,8},{8,9},{9,10},{10,1... | collective-permute-start | bytes 23048 | tf_op jit(solution)/shard_map/ppermute | solution.py:18
  49.2 6.8 %collective-permute-start.4 = (f32[8,4,6,10,1]{3,0,4,2,1:T(8,128)}, f32[8,4,6,10,1]{3,0,4,2,1:T(8,128)S(1)}, u32[]{:S(2)}, u32[]{:S(2)}) collective-permute-start(f32[8,4,6,10,1]{3,0,4,2,1:T(8,128)} %copy.34), channel_id=1, source_target_pairs={{1,0},{2,1},{3,2},{4,3},{5,4},{6,5},{7,6},{8,7},{9,8},{10,9},{11,1... | collective-permute-start | bytes 23048 | tf_op jit(solution)/shard_map/ppermute | solution.py:21
  77.4 36.7 %copy-start.5 = (f32[3,4,8,128]{3,2,1,0:T(8,128)S(1)}, f32[3,4,8,128]{3,2,1,0:T(8,128)}, u32[]{:S(2)}) copy-start(f32[3,4,8,128]{3,2,1,0:T(8,128)} %param.11) | copy-start | bytes 147460
  77.5 6.4 %collective-permute-start.7 = (f32[5,1,8,128]{3,2,1,0:T(8,128)S(1)}, f32[5,1,8,128]{3,2,1,0:T(8,128)S(1)}, u32[]{:S(2)}, u32[]{:S(2)}) collective-permute-start(f32[5,1,8,128]{3,2,1,0:T(8,128)S(1)} %get-tuple-element.164), channel_id=1, source_target_pairs={{0,64},{64,128},{128,192},{192,256},{256,320},{320,384},{384,448},... | collective-permute-start | bytes 61448 | tf_op jit(solution)/shard_map/ppermute | solution.py:18
  81.6 4.5 %collective-permute-start.6 = (f32[5,1,8,128]{3,2,1,0:T(8,128)S(1)}, f32[5,1,8,128]{3,2,1,0:T(8,128)S(1)}, u32[]{:S(2)}, u32[]{:S(2)}) collective-permute-start(f32[5,1,8,128]{3,2,1,0:T(8,128)S(1)} %get-tuple-element.165), channel_id=1, source_target_pairs={{64,0},{128,64},{192,128},{256,192},{320,256},{384,320},{448,384},... | collective-permute-start | bytes 61448 | tf_op jit(solution)/shard_map/ppermute | solution.py:21
  86.1 7.3 %collective-permute-start.9 = (f32[5,6,1,128]{3,2,1,0:T(1,128)S(1)}, f32[5,6,1,128]{3,2,1,0:T(1,128)S(1)}, u32[]{:S(2)}, u32[]{:S(2)}) collective-permute-start(f32[5,6,1,128]{3,2,1,0:T(1,128)S(1)} %get-tuple-element.148), channel_id=1, source_target_pairs={{0,16},{16,32},{32,48},{1,17},{17,33},{33,49},{2,18},{18,34},{34,5... | collective-permute-start | bytes 46088 | tf_op jit(solution)/shard_map/ppermute | solution.py:18
  91.4 6.6 %collective-permute-start.8 = (f32[5,6,1,128]{3,2,1,0:T(1,128)S(1)}, f32[5,6,1,128]{3,2,1,0:T(1,128)S(1)}, u32[]{:S(2)}, u32[]{:S(2)}) collective-permute-start(f32[5,6,1,128]{3,2,1,0:T(1,128)S(1)} %get-tuple-element.149), channel_id=1, source_target_pairs={{16,0},{32,16},{48,32},{17,1},{33,17},{49,33},{18,2},{34,18},{50,3... | collective-permute-start | bytes 46088 | tf_op jit(solution)/shard_map/ppermute | solution.py:21
  98.1 8.2 %collective-permute-start.10 = (f32[5,6,10,1]{3,2,1,0:T(8,128)S(1)}, f32[5,6,10,1]{3,2,1,0:T(8,128)S(1)}, u32[]{:S(2)}, u32[]{:S(2)}) collective-permute-start(f32[5,6,10,1]{3,2,1,0:T(8,128)S(1)} %get-tuple-element.108), channel_id=1, source_target_pairs={{1,0},{2,1},{3,2},{4,3},{5,4},{6,5},{7,6},{8,7},{9,8},{10,9},{11,1... | collective-permute-start | bytes 3608 | tf_op jit(solution)/shard_map/ppermute | solution.py:21
  100.1 7.7 %collective-permute-start.11 = (f32[5,6,10,1]{3,2,1,0:T(8,128)S(1)}, f32[5,6,10,1]{3,2,1,0:T(8,128)S(1)}, u32[]{:S(2)}, u32[]{:S(2)}) collective-permute-start(f32[5,6,10,1]{3,2,1,0:T(8,128)S(1)} %get-tuple-element.109), channel_id=1, source_target_pairs={{0,1},{1,2},{2,3},{3,4},{4,5},{5,6},{6,7},{7,8},{8,9},{9,10},{10,1... | collective-permute-start | bytes 3608 | tf_op jit(solution)/shard_map/ppermute | solution.py:18
  108.0 6.9 %collective-permute-start.13 = (f32[5,1,8,128]{3,2,1,0:T(8,128)S(1)}, f32[5,1,8,128]{3,2,1,0:T(8,128)S(1)}, u32[]{:S(2)}, u32[]{:S(2)}) collective-permute-start(f32[5,1,8,128]{3,2,1,0:T(8,128)S(1)} %get-tuple-element.162), channel_id=1, source_target_pairs={{0,64},{64,128},{128,192},{192,256},{256,320},{320,384},{384,448},... | collective-permute-start | bytes 61448 | tf_op jit(solution)/shard_map/ppermute | solution.py:18
  111.9 4.5 %collective-permute-start.12 = (f32[5,1,8,128]{3,2,1,0:T(8,128)S(1)}, f32[5,1,8,128]{3,2,1,0:T(8,128)S(1)}, u32[]{:S(2)}, u32[]{:S(2)}) collective-permute-start(f32[5,1,8,128]{3,2,1,0:T(8,128)S(1)} %get-tuple-element.163), channel_id=1, source_target_pairs={{64,0},{128,64},{192,128},{256,192},{320,256},{384,320},{448,384},... | collective-permute-start | bytes 61448 | tf_op jit(solution)/shard_map/ppermute | solution.py:21
  116.5 7.1 %collective-permute-start.15 = (f32[5,6,1,128]{3,2,1,0:T(1,128)S(1)}, f32[5,6,1,128]{3,2,1,0:T(1,128)S(1)}, u32[]{:S(2)}, u32[]{:S(2)}) collective-permute-start(f32[5,6,1,128]{3,2,1,0:T(1,128)S(1)} %get-tuple-element.146), channel_id=1, source_target_pairs={{0,16},{16,32},{32,48},{1,17},{17,33},{33,49},{2,18},{18,34},{34,5... | collective-permute-start | bytes 46088 | tf_op jit(solution)/shard_map/ppermute | solution.py:18
  121.6 6.6 %collective-permute-start.14 = (f32[5,6,1,128]{3,2,1,0:T(1,128)S(1)}, f32[5,6,1,128]{3,2,1,0:T(1,128)S(1)}, u32[]{:S(2)}, u32[]{:S(2)}) collective-permute-start(f32[5,6,1,128]{3,2,1,0:T(1,128)S(1)} %get-tuple-element.147), channel_id=1, source_target_pairs={{16,0},{32,16},{48,32},{17,1},{33,17},{49,33},{18,2},{34,18},{50,3... | collective-permute-start | bytes 46088 | tf_op jit(solution)/shard_map/ppermute | solution.py:21
  128.3 11.6 %collective-permute-start.16 = (f32[5,6,10,1]{3,2,1,0:T(8,128)S(1)}, f32[5,6,10,1]{3,2,1,0:T(8,128)S(1)}, u32[]{:S(2)}, u32[]{:S(2)}) collective-permute-start(f32[5,6,10,1]{3,2,1,0:T(8,128)S(1)} %get-tuple-element.106), channel_id=1, source_target_pairs={{1,0},{2,1},{3,2},{4,3},{5,4},{6,5},{7,6},{8,7},{9,8},{10,9},{11,1... | collective-permute-start | bytes 3608 | tf_op jit(solution)/shard_map/ppermute | solution.py:21
  130.3 9.7 %collective-permute-start.17 = (f32[5,6,10,1]{3,2,1,0:T(8,128)S(1)}, f32[5,6,10,1]{3,2,1,0:T(8,128)S(1)}, u32[]{:S(2)}, u32[]{:S(2)}) collective-permute-start(f32[5,6,10,1]{3,2,1,0:T(8,128)S(1)} %get-tuple-element.107), channel_id=1, source_target_pairs={{0,1},{1,2},{2,3},{3,4},{4,5},{5,6},{6,7},{7,8},{8,9},{9,10},{10,1... | collective-permute-start | bytes 3608 | tf_op jit(solution)/shard_map/ppermute | solution.py:18
  135.6 10.8 %collective-permute-start.32 = (f32[3,6,1,128]{3,2,1,0:T(1,128)S(1)}, f32[3,6,1,128]{3,2,1,0:T(1,128)S(1)}, u32[]{:S(2)}, u32[]{:S(2)}) collective-permute-start(f32[3,6,1,128]{3,2,1,0:T(1,128)S(1)} %get-tuple-element.169), channel_id=1, source_target_pairs={{0,16},{16,32},{32,48},{1,17},{17,33},{33,49},{2,18},{18,34},{34,5... | collective-permute-start | bytes 27656 | tf_op jit(solution)/shard_map/ppermute | solution.py:18
  137.8 8.5 %collective-permute-start.33 = (f32[3,6,1,128]{3,2,1,0:T(1,128)S(1)}, f32[3,6,1,128]{3,2,1,0:T(1,128)S(1)}, u32[]{:S(2)}, u32[]{:S(2)}) collective-permute-start(f32[3,6,1,128]{3,2,1,0:T(1,128)S(1)} %get-tuple-element.170), channel_id=1, source_target_pairs={{16,0},{32,16},{48,32},{17,1},{33,17},{49,33},{18,2},{34,18},{50,3... | collective-permute-start | bytes 27656 | tf_op jit(solution)/shard_map/ppermute | solution.py:21
  140.2 6.3 %collective-permute-start.19 = (f32[5,1,8,128]{3,2,1,0:T(8,128)S(1)}, f32[5,1,8,128]{3,2,1,0:T(8,128)S(1)}, u32[]{:S(2)}, u32[]{:S(2)}) collective-permute-start(f32[5,1,8,128]{3,2,1,0:T(8,128)S(1)} %get-tuple-element.160), channel_id=1, source_target_pairs={{0,64},{64,128},{128,192},{192,256},{256,320},{320,384},{384,448},... | collective-permute-start | bytes 61448 | tf_op jit(solution)/shard_map/ppermute | solution.py:18
  143.3 4.9 %collective-permute-start.18 = (f32[5,1,8,128]{3,2,1,0:T(8,128)S(1)}, f32[5,1,8,128]{3,2,1,0:T(8,128)S(1)}, u32[]{:S(2)}, u32[]{:S(2)}) collective-permute-start(f32[5,1,8,128]{3,2,1,0:T(8,128)S(1)} %get-tuple-element.161), channel_id=1, source_target_pairs={{64,0},{128,64},{192,128},{256,192},{320,256},{384,320},{448,384},... | collective-permute-start | bytes 61448 | tf_op jit(solution)/shard_map/ppermute | solution.py:21
  148.3 14.2 %collective-permute-start.21 = (f32[5,6,1,128]{3,2,1,0:T(1,128)S(1)}, f32[5,6,1,128]{3,2,1,0:T(1,128)S(1)}, u32[]{:S(2)}, u32[]{:S(2)}) collective-permute-start(f32[5,6,1,128]{3,2,1,0:T(1,128)S(1)} %get-tuple-element.144), channel_id=1, source_target_pairs={{0,16},{16,32},{32,48},{1,17},{17,33},{33,49},{2,18},{18,34},{34,5... | collective-permute-start | bytes 46088 | tf_op jit(solution)/shard_map/ppermute | solution.py:18
  154.9 7.6 %collective-permute-start.20 = (f32[5,6,1,128]{3,2,1,0:T(1,128)S(1)}, f32[5,6,1,128]{3,2,1,0:T(1,128)S(1)}, u32[]{:S(2)}, u32[]{:S(2)}) collective-permute-start(f32[5,6,1,128]{3,2,1,0:T(1,128)S(1)} %get-tuple-element.145), channel_id=1, source_target_pairs={{16,0},{32,16},{48,32},{17,1},{33,17},{49,33},{18,2},{34,18},{50,3... | collective-permute-start | bytes 46088 | tf_op jit(solution)/shard_map/ppermute | solution.py:21
  156.9 22.1 %collective-permute-start.34 = (f32[3,6,10,1]{3,2,1,0:T(8,128)S(1)}, f32[3,6,10,1]{3,2,1,0:T(8,128)S(1)}, u32[]{:S(2)}, u32[]{:S(2)}) collective-permute-start(f32[3,6,10,1]{3,2,1,0:T(8,128)S(1)} %get-tuple-element.140), channel_id=1, source_target_pairs={{0,1},{1,2},{2,3},{3,4},{4,5},{5,6},{6,7},{7,8},{8,9},{9,10},{10,1... | collective-permute-start | bytes 2168 | tf_op jit(solution)/shard_map/ppermute | solution.py:18
  160.6 18.5 %collective-permute-start.35 = (f32[3,6,10,1]{3,2,1,0:T(8,128)S(1)}, f32[3,6,10,1]{3,2,1,0:T(8,128)S(1)}, u32[]{:S(2)}, u32[]{:S(2)}) collective-permute-start(f32[3,6,10,1]{3,2,1,0:T(8,128)S(1)} %get-tuple-element.141), channel_id=1, source_target_pairs={{1,0},{2,1},{3,2},{4,3},{5,4},{6,5},{7,6},{8,7},{9,8},{10,9},{11,1... | collective-permute-start | bytes 2168 | tf_op jit(solution)/shard_map/ppermute | solution.py:21
  162.7 8.3 %collective-permute-start.22 = (f32[5,6,10,1]{3,2,1,0:T(8,128)S(1)}, f32[5,6,10,1]{3,2,1,0:T(8,128)S(1)}, u32[]{:S(2)}, u32[]{:S(2)}) collective-permute-start(f32[5,6,10,1]{3,2,1,0:T(8,128)S(1)} %get-tuple-element.104), channel_id=1, source_target_pairs={{1,0},{2,1},{3,2},{4,3},{5,4},{6,5},{7,6},{8,7},{9,8},{10,9},{11,1... | collective-permute-start | bytes 3608 | tf_op jit(solution)/shard_map/ppermute | solution.py:21
  164.6 7.7 %collective-permute-start.23 = (f32[5,6,10,1]{3,2,1,0:T(8,128)S(1)}, f32[5,6,10,1]{3,2,1,0:T(8,128)S(1)}, u32[]{:S(2)}, u32[]{:S(2)}) collective-permute-start(f32[5,6,10,1]{3,2,1,0:T(8,128)S(1)} %get-tuple-element.105), channel_id=1, source_target_pairs={{0,1},{1,2},{2,3},{3,4},{4,5},{5,6},{6,7},{7,8},{8,9},{9,10},{10,1... | collective-permute-start | bytes 3608 | tf_op jit(solution)/shard_map/ppermute | solution.py:18
  172.5 6.8 %collective-permute-start.25 = (f32[5,1,8,128]{3,2,1,0:T(8,128)S(1)}, f32[5,1,8,128]{3,2,1,0:T(8,128)S(1)}, u32[]{:S(2)}, u32[]{:S(2)}) collective-permute-start(f32[5,1,8,128]{3,2,1,0:T(8,128)S(1)} %get-tuple-element.158), channel_id=1, source_target_pairs={{0,64},{64,128},{128,192},{192,256},{256,320},{320,384},{384,448},... | collective-permute-start | bytes 61448 | tf_op jit(solution)/shard_map/ppermute | solution.py:18
  175.7 27.5 %copy-start.4 = (f32[3,4,4,8,128]{4,3,2,1,0:T(8,128)S(1)}, f32[3,4,4,8,128]{4,3,2,1,0:T(8,128)}, u32[]{:S(2)}) copy-start(f32[3,4,4,8,128]{4,3,2,1,0:T(8,128)} %param.10) | copy-start | bytes 589828
  175.7 27.5 %copy-start.6 = (f32[4,4,8,128]{3,2,1,0:T(8,128)S(1)}, f32[4,4,8,128]{3,2,1,0:T(8,128)}, u32[]{:S(2)}) copy-start(f32[4,4,8,128]{3,2,1,0:T(8,128)} %get-tuple-element.122) | copy-start | bytes 196612
  175.7 27.5 %copy-start.7 = (f32[4,4,8,128]{3,2,1,0:T(8,128)S(1)}, f32[4,4,8,128]{3,2,1,0:T(8,128)}, u32[]{:S(2)}) copy-start(f32[4,4,8,128]{3,2,1,0:T(8,128)} %get-tuple-element.123) | copy-start | bytes 196612
  175.7 27.5 %copy-start.8 = (f32[4,4,8,128]{3,2,1,0:T(8,128)S(1)}, f32[4,4,8,128]{3,2,1,0:T(8,128)}, u32[]{:S(2)}) copy-start(f32[4,4,8,128]{3,2,1,0:T(8,128)} %get-tuple-element.124) | copy-start | bytes 196612
  175.7 27.5 %copy-start.9 = (f32[4,4,8,128]{3,2,1,0:T(8,128)S(1)}, f32[4,4,8,128]{3,2,1,0:T(8,128)}, u32[]{:S(2)}) copy-start(f32[4,4,8,128]{3,2,1,0:T(8,128)} %get-tuple-element.125) | copy-start | bytes 196612
  175.7 27.5 %copy-start.10 = (f32[4,4,8,128]{3,2,1,0:T(8,128)S(1)}, f32[4,4,8,128]{3,2,1,0:T(8,128)}, u32[]{:S(2)}) copy-start(f32[4,4,8,128]{3,2,1,0:T(8,128)} %get-tuple-element.126) | copy-start | bytes 196612
  175.7 27.5 %copy-start.11 = (f32[4,4,8,128]{3,2,1,0:T(8,128)S(1)}, f32[4,4,8,128]{3,2,1,0:T(8,128)}, u32[]{:S(2)}) copy-start(f32[4,4,8,128]{3,2,1,0:T(8,128)} %get-tuple-element.127) | copy-start | bytes 196612
  175.7 27.5 %copy-start.12 = (f32[4,4,8,128]{3,2,1,0:T(8,128)S(1)}, f32[4,4,8,128]{3,2,1,0:T(8,128)}, u32[]{:S(2)}) copy-start(f32[4,4,8,128]{3,2,1,0:T(8,128)} %get-tuple-element.110) | copy-start | bytes 196612
  175.8 27.5 %copy-start.13 = (f32[4,4,8,128]{3,2,1,0:T(8,128)S(1)}, f32[4,4,8,128]{3,2,1,0:T(8,128)}, u32[]{:S(2)}) copy-start(f32[4,4,8,128]{3,2,1,0:T(8,128)} %get-tuple-element.111) | copy-start | bytes 196612
  175.8 27.5 %copy-start.14 = (f32[4,4,8,128]{3,2,1,0:T(8,128)S(1)}, f32[4,4,8,128]{3,2,1,0:T(8,128)}, u32[]{:S(2)}) copy-start(f32[4,4,8,128]{3,2,1,0:T(8,128)} %get-tuple-element.112) | copy-start | bytes 196612
  175.8 27.5 %copy-start.15 = (f32[4,4,8,128]{3,2,1,0:T(8,128)S(1)}, f32[4,4,8,128]{3,2,1,0:T(8,128)}, u32[]{:S(2)}) copy-start(f32[4,4,8,128]{3,2,1,0:T(8,128)} %get-tuple-element.113) | copy-start | bytes 196612
  175.9 4.7 %collective-permute-start.24 = (f32[5,1,8,128]{3,2,1,0:T(8,128)S(1)}, f32[5,1,8,128]{3,2,1,0:T(8,128)S(1)}, u32[]{:S(2)}, u32[]{:S(2)}) collective-permute-start(f32[5,1,8,128]{3,2,1,0:T(8,128)S(1)} %get-tuple-element.159), channel_id=1, source_target_pairs={{64,0},{128,64},{192,128},{256,192},{320,256},{384,320},{448,384},... | collective-permute-start | bytes 61448 | tf_op jit(solution)/shard_map/ppermute | solution.py:21
  180.6 10.7 %collective-permute-start.27 = (f32[5,6,1,128]{3,2,1,0:T(1,128)S(1)}, f32[5,6,1,128]{3,2,1,0:T(1,128)S(1)}, u32[]{:S(2)}, u32[]{:S(2)}) collective-permute-start(f32[5,6,1,128]{3,2,1,0:T(1,128)S(1)} %get-tuple-element.142), channel_id=1, source_target_pairs={{0,16},{16,32},{32,48},{1,17},{17,33},{33,49},{2,18},{18,34},{34,5... | collective-permute-start | bytes 46088 | tf_op jit(solution)/shard_map/ppermute | solution.py:18
  189.2 6.6 %collective-permute-start.26 = (f32[5,6,1,128]{3,2,1,0:T(1,128)S(1)}, f32[5,6,1,128]{3,2,1,0:T(1,128)S(1)}, u32[]{:S(2)}, u32[]{:S(2)}) collective-permute-start(f32[5,6,1,128]{3,2,1,0:T(1,128)S(1)} %get-tuple-element.143), channel_id=1, source_target_pairs={{16,0},{32,16},{48,32},{17,1},{33,17},{49,33},{18,2},{34,18},{50,3... | collective-permute-start | bytes 46088 | tf_op jit(solution)/shard_map/ppermute | solution.py:21
  195.9 8.9 %collective-permute-start.28 = (f32[5,6,10,1]{3,2,1,0:T(8,128)S(1)}, f32[5,6,10,1]{3,2,1,0:T(8,128)S(1)}, u32[]{:S(2)}, u32[]{:S(2)}) collective-permute-start(f32[5,6,10,1]{3,2,1,0:T(8,128)S(1)} %get-tuple-element.102), channel_id=1, source_target_pairs={{1,0},{2,1},{3,2},{4,3},{5,4},{6,5},{7,6},{8,7},{9,8},{10,9},{11,1... | collective-permute-start | bytes 3608 | tf_op jit(solution)/shard_map/ppermute | solution.py:21
  197.8 8.4 %collective-permute-start.29 = (f32[5,6,10,1]{3,2,1,0:T(8,128)S(1)}, f32[5,6,10,1]{3,2,1,0:T(8,128)S(1)}, u32[]{:S(2)}, u32[]{:S(2)}) collective-permute-start(f32[5,6,10,1]{3,2,1,0:T(8,128)S(1)} %get-tuple-element.103), channel_id=1, source_target_pairs={{0,1},{1,2},{2,3},{3,4},{4,5},{5,6},{6,7},{7,8},{8,9},{9,10},{10,1... | collective-permute-start | bytes 3608 | tf_op jit(solution)/shard_map/ppermute | solution.py:18
  (13 other events, 277.1 us)
where the time goes:
time: 209 us; the launch traced here: 207 us
  starting transfers between devices  124 us (59%)
  waiting for transfers between devices  37.1 us (18%)
  other arithmetic  29.9 us (14%)
  local copies, waits for them, and re-layouts  14.3 us (7%)
    ppermute x18, starting transfers between devices, padded_2(): lax.ppermute(lax.slice_in_dim(block, block.shape[dim] - width, None, axis...  85.2 us
    ppermute x18, starting transfers between devices, padded_2(): lax.ppermute(lax.slice_in_dim(block, 0, width, axis=dim), axis, backward)  38.9 us
    ppermute x18, waiting for transfers between devices, padded_2(): lax.ppermute(lax.slice_in_dim(block, 0, width, axis=dim), axis, backward)  32.7 us
    concatenate x16, other arithmetic, padded_2(): block = jnp.concatenate([low, block, high], axis=dim)  10.8 us
    reduce_sum x4, other arithmetic, deposit_owner(): jnp.sum(padded_sources[(slice(None), slice(None)) + window] * factor[None...  5.71 us
    ppermute x18, waiting for transfers between devices, padded_2(): lax.ppermute(lax.slice_in_dim(block, block.shape[dim] - width, None, axis...  4.33 us
    slice x7, local copies, waits for them, and re-layouts, padded_2(): lax.slice_in_dim(block, 0, width, axis=dim)  4.3 us
  transfers between devices with their start and end apart: 36, of which 16 were waited for; matrix products, arithmetic and copies ran while one was open for 20% of the time, Pallas kernels for 0%

commit v1 on v0

v1 whole, which is shorter than its diff:
```python
import functools
import math

import jax
import jax.numpy as jnp
from jax import lax
from jax.experimental import pallas as pl
from jax.experimental.pallas import tpu as pltpu
from jax.sharding import PartitionSpec as P

MESH = pl.DeviceIdType.MESH
F32 = jnp.float32
SIGMA = 0.6
INV_S2 = 1.0 / (SIGMA * SIGMA)
CENTRE = math.exp(0.5 * INV_S2)

DIAG = ((-1, -1), (-1, 1), (1, -1), (1, 1))
ALL = ([(0, a, b) for a in (-1, 0, 1) for b in (-1, 0, 1) if (a, b) != (0, 0)]
       + [(-1, 0, 0), (1, 0, 0), (-2, 0, 0), (2, 0, 0)])


def rot(value, shift, axis):
    size = value.shape[axis]
    return pltpu.roll(value, shift % size, axis)


def kernel(sizes, counts_h, offsets_h, volume_h, beta_h, pv_h, gas_h, filtered_h, drag_h,
           counts_v, offsets_v, src_v, pv_v, gas_v, occ_v, prod_v, shifted_v,
           dm_v, dy_v, dz_v, dyz_v, mx_v, mxy_v,
           sy_v, sz_v, sd_v, ry_v, rz_v, rd_v,
           sgy_v, sgz_v, rgy_v, rgz_v, rgd_v,
           fx_v, fx2_v, rx_v, rx2_v, out_v, drag_v,
           in_sem, out_sem, y_ss, y_rs, z_ss, z_rs, d_ss, d_rs,
           gx_ss, gx_rs, gy_ss, gy_rs, gz_ss, gz_rs, gd_ss, gd_rs, x_ss, x_rs, x2_ss, x2_rs):
    me = (lax.axis_index("gx"), lax.axis_index("gy"), lax.axis_index("gz"))

    def near(step):
        place = tuple(me[i] + step[i] for i in range(3))
        ok = None
        for i in range(3):
            if step[i]:
                inside = (place[i] >= 0) & (place[i] < sizes[i])
                ok = inside if ok is None else ok & inside
        return place, ok

    def send(step, src, dst, ssem, rsem):
        place, ok = near(step)

        @pl.when(ok)
        def _():
            pltpu.make_async_remote_copy(src_ref=src, dst_ref=dst, send_sem=ssem, recv_sem=rsem,
                                         device_id=place, device_id_type=MESH).start()

    def wait_recv(step, src, dst, ssem, rsem):
        place, ok = near(step)

        @pl.when(ok)
        def _():
            pltpu.make_async_remote_copy(src_ref=src, dst_ref=dst, send_sem=ssem, recv_sem=rsem,
                                         device_id=place, device_id_type=MESH).wait_recv()

    def wait_send(step, src, dst, ssem, rsem):
        place, ok = near(step)

        @pl.when(ok)
        def _():
            pltpu.make_async_remote_copy(src_ref=src, dst_ref=dst, send_sem=ssem, recv_sem=rsem,
                                         device_id=place, device_id_type=MESH).wait_send()

    loads = [
        pltpu.make_async_copy(gas_h, gas_v.at[:, pl.ds(1, 4)], in_sem.at[0]),
        pltpu.make_async_copy(counts_h, counts_v, in_sem.at[1]),
        pltpu.make_async_copy(offsets_h, offsets_v, in_sem.at[2]),
        pltpu.make_async_copy(volume_h, src_v.at[0], in_sem.at[3]),
        pltpu.make_async_copy(beta_h, src_v.at[1], in_sem.at[4]),
        pltpu.make_async_copy(pv_h, pv_v, in_sem.at[5]),
    ]
    for load in loads:
        load.start()
    barrier = pltpu.get_barrier_semaphore()
    greeted = jnp.int32(0)
    for step in ALL:
        place, ok = near(step)
        greeted = greeted + ok.astype(jnp.int32)

        @pl.when(ok)
        def _():
            pl.semaphore_signal(barrier, inc=1, device_id=place, device_id_type=MESH)

    def clear(step, refs):
        _, ok = near(step)

        @pl.when(jnp.logical_not(ok))
        def _():
            for ref in refs:
                ref[...] = jnp.zeros(ref.shape, F32)

    for n, s in enumerate((-1, 1)):
        clear((s, 0, 0), [gas_v.at[:, 5 * n], rx_v.at[n]])
        clear((2 * s, 0, 0), [rx2_v.at[n]])
        clear((0, s, 0), [ry_v.at[n], rgy_v.at[n]])
        clear((0, 0, s), [rz_v.at[n], rgz_v.at[n]])
    for n, (a, b) in enumerate(DIAG):
        clear((0, a, b), [rd_v.at[n], rgd_v.at[n]])

    row = lax.broadcasted_iota(jnp.int32, (8, 128), 0)
    lane = lax.broadcasted_iota(jnp.int32, (8, 128), 1)
    slot, col = lane >> 3, lane & 7
    row0, row7, row_low = row == 0, row == 7, row < 4
    lane0, lane127, col_low = lane == 0, lane == 127, col < 4
    col3, col4 = col == 3, col == 4

    coef = F32(2.0 / 13.0)
    plane = lax.broadcasted_iota(jnp.int32, (14, 8, 128), 0) + (4 * me[0] - 5)
    in_x = jnp.where((plane >= 0) & (plane < 4 * sizes[0]), coef, 0.0)
    row_ok = jnp.where(row_low, (me[1] < sizes[1] - 1).astype(F32), (me[1] > 0).astype(F32))
    mx_v[...] = in_x
    mxy_v[...] = in_x * row_ok[None]
    slot_plane = slot + (4 * me[0] - 5)
    cz = jnp.where((slot_plane >= 0) & (slot_plane < 4 * sizes[0]), coef, 0.0) * jnp.where(
        col_low, (me[2] > 0).astype(F32), (me[2] < sizes[2] - 1).astype(F32))
    cyz = cz * row_ok

    loads[0].wait()
    pl.semaphore_wait(barrier, greeted)
    gas_x = [((-1, 0, 0), gas_v.at[:, 1], gas_v.at[:, 5], gx_ss.at[0], gx_rs.at[1]),
             ((1, 0, 0), gas_v.at[:, 4], gas_v.at[:, 0], gx_ss.at[1], gx_rs.at[0])]
    for item in gas_x:
        send(*item)

    loads[1].wait()
    loads[2].wait()

    def products(s, carry):
        occ = jnp.where(counts_v[...] > s, F32(1.0), F32(0.0))
        occ_v[s] = occ
        weights, norm = [], None
        for axis in range(3):
            t = jnp.exp((0.5 - offsets_v[axis, s]) * INV_S2)
            low, mid = t * t, CENTRE * t
            total = low + mid + 1.0
            norm = total if norm is None else norm * total
            weights.append((low, mid))
        scale = occ / norm
        wx = (weights[0][0] * scale, weights[0][1] * scale, scale)
        for a in range(3):
            for b in range(3):
                xy = wx[a] * weights[1][b] if b < 2 else wx[a]
                for c in range(3):
                    prod_v[9 * a + 3 * b + c, s] = xy * weights[2][c] if c < 2 else xy
        return carry

    lax.fori_loop(0, 4, products, 0)
    for load in loads[3:]:
        load.wait()
    for j in range(3):
        src_v[2 + j] = src_v[1] * pv_v[j]

    def pack(planes, first):
        result = jnp.zeros((8, 128), F32)
        for i in range(planes.shape[0]):
            result = jnp.where(slot == first + i, rot(planes[i], 8 * (first + i) + 4, 1), result)
        return result

    def unpack(tile, first, count):
        return jnp.stack([rot(tile, -(8 * (first + i) + 4), 1) for i in range(count)])

    def y_copy(n, k):
        return ((0, (-1, 1)[n], 0), sy_v.at[n, k], ry_v.at[1 - n, k], y_ss.at[n, k], y_rs.at[1 - n, k])

    def deposit(k, carry):
        src = [src_v[k, s] for s in range(4)]
        mz, zz = [], []
        for b in range(3):
            by_z = []
            for c in range(3):
                by_x = []
                for a in range(3):
                    total = src[0] * prod_v[9 * a + 3 * b + c, 0]
                    for s in range(1, 4):
                        total = total + src[s] * prod_v[9 * a + 3 * b + c, s]
                    by_x.append(total)
                lo, mid, hi = by_x
                by_z.append(jnp.concatenate([
                    lo[0:1], lo[1:2] + mid[0:1], lo[2:4] + mid[1:3] + hi[0:2], mid[3:4] + hi[2:3], hi[3:4]], axis=0))
            up, down = rot(by_z[2], 1, 2), rot(by_z[0], -1, 2)
            mz.append(by_z[1] + jnp.where(lane0[None], 0.0, up) + jnp.where(lane127[None], 0.0, down))
            spill = jnp.where(lane0[None], up, jnp.where(lane127[None], down, 0.0))
            packed = rot(spill[0], 36, 1)
            for i in range(1, 6):
                packed = packed + rot(spill[i], 8 * i + 36, 1)
            zz.append(packed)
        up, down = rot(mz[2], 1, 1), rot(mz[0], -1, 1)
        m = mz[1] + jnp.where(row0[None], 0.0, up) + jnp.where(row7[None], 0.0, down)
        y = jnp.where(row0[None], up, jnp.where(row7[None], down, 0.0))
        up, down = rot(zz[2], 1, 0), rot(zz[0], -1, 0)
        z = zz[1] + jnp.where(row0, 0.0, up) + jnp.where(row7, 0.0, down)
        yz = jnp.where(row0, up, jnp.where(row7, down, 0.0))
        dm_v[k], dy_v[k], dz_v[k], dyz_v[k] = m, y, z, yz
        sy_v[0, k, 0:6] = jnp.where(row_low[None], m, y)
        sy_v[1, k, 0:6] = jnp.where(row_low[None], y, m)
        sy_v[0, k, 6] = jnp.where(row_low, z, yz)
        sy_v[1, k, 6] = jnp.where(row_low, yz, z)
        for n in range(2):
            send(*y_copy(n, k))
        mp, yp = pack(m, 4), pack(y, 4)
        zm = (jnp.where(col_low, z, mp), jnp.where(col_low, mp, z))
        zy = (jnp.where(col_low, yz, yp), jnp.where(col_low, yp, yz))
        for n in range(2):
            sz_v[n, k, 0], sz_v[n, k, 1] = zm[n], zy[n]
        for n, (a, b) in enumerate(DIAG):
            first, second = (zm, zy) if a < 0 else (zy, zm)
            sd_v[n, k] = jnp.where(row_low, first[(b + 1) // 2], second[(b + 1) // 2])
        return carry

    lax.fori_loop(0, 5, deposit, 0)
    z_copies = [((0, 0, s), sz_v.at[n], rz_v.at[1 - n], z_ss.at[n], z_rs.at[1 - n]) for n, s in enumerate((-1, 1))]
    d_copies = [((0, a, b), sd_v.at[n], rd_v.at[3 - n], d_ss.at[n], d_rs.at[3 - n]) for n, (a, b) in enumerate(DIAG)]
    for item in d_copies + z_copies:
        send(*item)

    for item in gas_x:
        wait_recv(item[0], item[1], gas_v.at[:, 0 if item[0][0] < 0 else 5], item[3], gx_rs.at[0 if item[0][0] < 0 else 1])
    for j in range(3):
        sgz_v[j] = pack(gas_v[j], 4)
        for i in range(6):
            sgy_v[0, j, pl.ds(i, 1), :] = gas_v[j, i, pl.ds(0, 1), :]
            sgy_v[1, j, pl.ds(i, 1), :] = gas_v[j, i, pl.ds(7, 1), :]
        for n in range(2):
            sgy_v[n, j, pl.ds(6, 2), :] = jnp.zeros((2, 128), F32)
    gy_copies = [((0, s, 0), sgy_v.at[n], rgy_v.at[1 - n], gy_ss.at[n], gy_rs.at[1 - n]) for n, s in enumerate((-1, 1))]
    gz_copies = [((0, 0, s), sgz_v, rgz_v.at[1 - n], gz_ss.at[n], gz_rs.at[1 - n]) for n, s in enumerate((-1, 1))]
    gd_copies = [((0, a, b), sgz_v, rgd_v.at[3 - n], gd_ss.at[n], gd_rs.at[3 - n]) for n, (a, b) in enumerate(DIAG)]
    for item in gy_copies + gz_copies + gd_copies:
        send(*item)

    for n, s in enumerate((-1, 1)):
        wait_recv((0, 0, s), sz_v.at[n], rz_v.at[n], z_ss.at[n], z_rs.at[n])
    for n, (a, b) in enumerate(DIAG):
        wait_recv((0, a, b), sd_v.at[n], rd_v.at[n], d_ss.at[n], d_rs.at[n])

    def x_copies(k):
        return [((-1, 0, 0), fx_v.at[0, k], rx_v.at[1, k], x_ss.at[0, k], x_rs.at[1, k]),
                ((1, 0, 0), fx_v.at[1, k], rx_v.at[0, k], x_ss.at[1, k], x_rs.at[0, k]),
                ((-2, 0, 0), fx2_v.at[0, k], rx2_v.at[1, k], x2_ss.at[0, k], x2_rs.at[1, k]),
                ((2, 0, 0), fx2_v.at[1, k], rx2_v.at[0, k], x2_ss.at[1, k], x2_rs.at[0, k])]

    def widen(cur):
        count = cur.shape[0]
        return jnp.concatenate([cur[0:1], cur[1:2], cur[0:count - 2] + cur[2:count],
                                cur[count - 2:count - 1], cur[count - 1:count]], axis=0)

    def z_sum(tiles, halo, first):
        edge = unpack(halo, first, tiles.shape[0])
        return (rot(jnp.where(lane0[None], edge, tiles), -1, 2) + rot(jnp.where(lane127[None], edge, tiles), 1, 2))

    def y_sum(tiles, halo):
        axis = tiles.ndim - 2
        return rot(jnp.where(row0, halo, tiles), -1, axis) + rot(jnp.where(row7, halo, tiles), 1, axis)

    def packed_sum(tile, edges):
        return (rot(tile, 8, 1) + rot(tile, -8, 1) + rot(jnp.where(col4, edges, tile), -1, 1)
                + rot(jnp.where(col3, edges, tile), 1, 1))

    def grow(total, inner):
        count = total.shape[0]
        return jnp.concatenate([total[0:1], total[1:count - 1] + inner, total[count - 1:count]], axis=0)

    def add_source(total, source, lead):
        count = total.shape[0]
        return jnp.concatenate([total[0:lead], total[lead:lead + 6] + source, total[lead + 6:count]], axis=0)

    def filter_one(k, carry):
        for n in range(2):
            s = (-1, 1)[n]
            wait_recv((0, s, 0), sy_v.at[n, k], ry_v.at[n, k], y_ss.at[n, k], y_rs.at[n, k])
        below, above = ry_v[0, k, 0:6], ry_v[1, k, 0:6]
        below_z, above_z = ry_v[0, k, 6], ry_v[1, k, 6]
        m = dm_v[k] + jnp.where(row_low[None], below, above)
        y = dy_v[k] + jnp.where(row_low[None], above, below)
        side = []
        for n, b in enumerate((0, 1)):
            lower, upper = rd_v[b, k], rd_v[2 + b, k]
            side.append((rz_v[n, k, 0] + jnp.where(row_low, lower, upper),
                         rz_v[n, k, 1] + jnp.where(row_low, upper, lower)))
        z = dz_v[k] + jnp.where(col_low, side[0][0], side[1][0]) + jnp.where(row_low, below_z, above_z)
        yz = dyz_v[k] + jnp.where(col_low, side[0][1], side[1][1]) + jnp.where(row_low, above_z, below_z)
        ends = (lane0 | lane127)[None]
        m = m + jnp.where(ends, unpack(jnp.where(col_low, side[1][0], side[0][0]), 4, 6), 0.0)
        y = y + jnp.where(ends, unpack(jnp.where(col_low, side[1][1], side[0][1]), 4, 6), 0.0)
        m13, y13 = m * (0.5 * mx_v[4:10]), y * (0.5 * mxy_v[4:10])
        z13, yz13 = z * (0.5 * cz), yz * (0.5 * cyz)
        cm, cy, cz_now, cyz_now = m13, y13, z13, yz13
        for sweep in range(1, 5):
            first = 5 - sweep
            gain = F32(13.0) if sweep == 1 else None
            scale_m = mx_v[first - 1:first + 5 + 2 * sweep]
            m_sum = grow(widen(cm), y_sum(cm, cy) + z_sum(cm, cz_now, first))
            if gain is not None:
                m_sum = m_sum * gain
            next_m = add_source(m_sum * scale_m, m13, sweep)
            if sweep < 4:
                scale_y = mxy_v[first - 1:first + 5 + 2 * sweep]
                y_total = grow(widen(cy), y_sum(cy, cm) + z_sum(cy, cyz_now, first))
                z_total = packed_sum(cz_now, pack(cm, first)) + y_sum(cz_now, cyz_now)
                yz_total = packed_sum(cyz_now, pack(cy, first)) + y_sum(cyz_now, cz_now)
                if gain is not None:
                    y_total, z_total, yz_total = y_total * gain, z_total * gain, yz_total * gain
                cy = add_source(y_total * scale_y, y13, sweep)
                cz_now, cyz_now = z13 + z_total * cz, yz13 + yz_total * cyz
            cm = next_m
        fx2_v[0, k] = cm[0]
        fx_v[0, k] = cm[1:5]
        out_v[k] = cm[5:9]
        fx_v[1, k] = cm[9:13]
        fx2_v[1, k] = cm[13]
        for item in x_copies(k):
            send(*item)
        return carry

    lax.fori_loop(0, 5, filter_one, 0)

    for n, s in enumerate((-1, 1)):
        wait_recv((0, s, 0), sgy_v.at[n], rgy_v.at[n], gy_ss.at[n], gy_rs.at[n])
        wait_recv((0, 0, s), sgz_v, rgz_v.at[n], gz_ss.at[n], gz_rs.at[n])
    for n, (a, b) in enumerate(DIAG):
        wait_recv((0, a, b), sgz_v, rgd_v.at[n], gd_ss.at[n], gd_rs.at[n])

    def shift(j, carry):
        tiles = gas_v[j]
        below, above = rgy_v[0, j], rgy_v[1, j]
        rows = jnp.stack([jnp.where(row0, jnp.broadcast_to(above[i:i + 1], (8, 128)),
                                    jnp.broadcast_to(below[i:i + 1], (8, 128))) for i in range(6)])
        halo_m = jnp.where(col_low, rgz_v[0, j], rgz_v[1, j])
        halo_y = jnp.where(col_low, jnp.where(row0, rgd_v[2, j], rgd_v[0, j]),
                           jnp.where(row0, rgd_v[3, j], rgd_v[1, j]))
        variants = []
        for value, halo in ((tiles, halo_m), (rows, halo_y)):
            edge = unpack(halo, 4, 6)
            variants.append((rot(jnp.where(lane127[None], edge, value), 1, 2), value,
                             rot(jnp.where(lane0[None], edge, value), -1, 2)))
        for c in range(3):
            value, halo = variants[0][c], variants[1][c]
            shifted_v[j, c] = rot(jnp.where(row7[None], halo, value), 1, 1)
            shifted_v[j, 3 + c] = value
            shifted_v[j, 6 + c] = rot(jnp.where(row0[None], halo, value), -1, 1)
        return carry

    lax.fori_loop(0, 3, shift, 0)

    def drag(x, carry):
        totals = [jnp.zeros((4, 8, 128), F32) for _ in range(3)]
        for a in range(3):
            for bc in range(9):
                weight = prod_v[9 * a + bc, :, x]
                for j in range(3):
                    totals[j] = totals[j] + weight * shifted_v[j, bc, x + a][None]
        for j in range(3):
            drag_v[j, :, x] = src_v[1, :, x] * totals[j] - occ_v[:, x] * src_v[2 + j, :, x]
        return carry

    lax.fori_loop(0, 4, drag, 0)
    drag_out = pltpu.make_async_copy(drag_v, drag_h, out_sem.at[0])
    drag_out.start()

    def finish(k, carry):
        for n in range(2):
            s = (-1, 1)[n]
            wait_recv((s, 0, 0), fx_v.at[n, k], rx_v.at[n, k], x_ss.at[n, k], x_rs.at[n, k])
            wait_recv((2 * s, 0, 0), fx2_v.at[n, k], rx2_v.at[n, k], x2_ss.at[n, k], x2_rs.at[n, k])
        total = out_v[k] + (rx_v[0, k] + rx_v[1, k])
        out_v[k] = jnp.concatenate([total[0:1] + rx2_v[0, k][None], total[1:3], total[3:4] + rx2_v[1, k][None]], axis=0)
        return carry

    lax.fori_loop(0, 5, finish, 0)
    filtered_out = pltpu.make_async_copy(out_v, filtered_h, out_sem.at[1])
    filtered_out.start()

    def sent(k, carry):
        for n in range(2):
            wait_send(*y_copy(n, k))
        for item in x_copies(k):
            wait_send(*item)
        return carry

    lax.fori_loop(0, 5, sent, 0)
    for item in gas_x + z_copies + d_copies + gy_copies + gz_copies + gd_copies:
        wait_send(*item)
    drag_out.wait()
    filtered_out.wait()


def solution(mesh):
    sizes = tuple(mesh.shape[name] for name in ("gx", "gy", "gz"))
    dma = pltpu.SemaphoreType.DMA

    def vmem(*shape):
        return pltpu.VMEM(shape + (8, 128), F32)

    def shards(counts, offsets, volume, beta, particle_velocity, gas_velocity):
        any_space = pl.BlockSpec(memory_space=pl.ANY)
        return pl.pallas_call(
            functools.partial(kernel, sizes),
            out_shape=(jax.ShapeDtypeStruct((5, 4, 8, 128), F32), jax.ShapeDtypeStruct((3, 4, 4, 8, 128), F32)),
            in_specs=[any_space] * 6,
            out_specs=(any_space, any_space),
            scratch_shapes=[
                pltpu.VMEM((4, 8, 128), jnp.int32), vmem(3, 4, 4), vmem(5, 4, 4), vmem(3, 4, 4), vmem(3, 6),
                vmem(4, 4), vmem(27, 4, 4), vmem(3, 9, 6),
                vmem(5, 6), vmem(5, 6), vmem(5), vmem(5), vmem(14), vmem(14),
                vmem(2, 5, 7), vmem(2, 5, 2), vmem(4, 5), vmem(2, 5, 7), vmem(2, 5, 2), vmem(4, 5),
                vmem(2, 3), vmem(3), vmem(2, 3), vmem(2, 3), vmem(4, 3),
                vmem(2, 5, 4), vmem(2, 5), vmem(2, 5, 4), vmem(2, 5), vmem(5, 4), vmem(3, 4, 4),
                dma((6,)), dma((2,)), dma((2, 5)), dma((2, 5)), dma((2,)), dma((2,)), dma((4,)), dma((4,)),
                dma((2,)), dma((2,)), dma((2,)), dma((2,)), dma((2,)), dma((2,)), dma((4,)), dma((4,)),
                dma((2, 5)), dma((2, 5)), dma((2, 5)), dma((2, 5)),
            ],
            compiler_params=pltpu.CompilerParams(
                collective_id=0, has_side_effects=True, vmem_limit_bytes=32 * 2**20),
            name="deposit_filter_drag",
        )(counts, offsets, volume, beta, particle_velocity, gas_velocity)

    in_specs = (
        P("gx", "gy", "gz"),
        P(None, None, "gx", "gy", "gz"),
        P(None, "gx", "gy", "gz"),
        P(None, "gx", "gy", "gz"),
        P(None, None, "gx", "gy", "gz"),
        P(None, "gx", "gy", "gz"),
    )
    out_specs = (P(None, "gx", "gy", "gz"), P(None, None, "gx", "gy", "gz"))
    return jax.shard_map(shards, mesh=mesh, in_specs=in_specs, out_specs=out_specs, check_vma=False)
```

time: 209 us -> 35 us (0.17)
  the two profiles are of different devices: /device:TPU:473 before, /device:TPU:1 now
where the time goes in v1:
time: 35 us; the launch traced here: 34.6 us
  Pallas kernels  27.6 us (79%)
  local copies, waits for them, and re-layouts  6.35 us (18%)
  between operations  0.65 us (2%)
    pallas_call x1, Pallas kernels, shards(): pl.pallas_call(functools.partial(kernel, sizes), out_shape=(jax.ShapeDtyp...  27.6 us
    unnamed x14, local copies, waits for them, and re-layouts  6.35 us

profile of v1, /device:TPU:1, one launch (start us, length us, event | category | flops | bytes accessed | tf_op | source)
XLA Modules:
  0.0 34.6 jit_solution(1318750433738962904)
XLA Ops:
  0.6 0.0 copy-start
  0.6 0.9 %copy-done = f32[3,4,4,8,128]{4,3,2,1,0:T(8,128)S(1)} copy-done((f32[3,4,4,8,128]{4,3,2,1,0:T(8,128)S(1)}, f32[3,4,4,8,128]{4,3,2,1,0:T(8,128)}, u32[]{:S(2)}) %copy-start) | copy-done | bytes 196632
  1.6 0.0 copy-start.1
  1.6 0.9 %copy-done.1 = f32[3,4,4,8,128]{4,3,2,1,0:T(8,128)S(1)} copy-done((f32[3,4,4,8,128]{4,3,2,1,0:T(8,128)S(1)}, f32[3,4,4,8,128]{4,3,2,1,0:T(8,128)}, u32[]{:S(2)}) %copy-start.1) | copy-done | bytes 196632
  2.5 0.0 copy-start.2
  2.5 0.8 %copy-done.2 = f32[4,4,8,128]{3,2,1,0:T(8,128)S(1)} copy-done((f32[4,4,8,128]{3,2,1,0:T(8,128)S(1)}, f32[4,4,8,128]{3,2,1,0:T(8,128)}, u32[]{:S(2)}) %copy-start.2) | copy-done | bytes 65560
  3.3 0.0 copy-start.3
  3.3 0.8 %copy-done.3 = f32[4,4,8,128]{3,2,1,0:T(8,128)S(1)} copy-done((f32[4,4,8,128]{3,2,1,0:T(8,128)S(1)}, f32[4,4,8,128]{3,2,1,0:T(8,128)}, u32[]{:S(2)}) %copy-start.3) | copy-done | bytes 65560
  4.2 0.0 copy-start.4
  4.2 0.8 %copy-done.4 = f32[3,4,8,128]{3,2,1,0:T(8,128)S(1)} copy-done((f32[3,4,8,128]{3,2,1,0:T(8,128)S(1)}, f32[3,4,8,128]{3,2,1,0:T(8,128)}, u32[]{:S(2)}) %copy-start.4) | copy-done | bytes 49176
  5.0 0.0 copy-start.5
  5.0 0.7 %copy-done.5 = s32[4,8,128]{2,1,0:T(8,128)S(1)} copy-done((s32[4,8,128]{2,1,0:T(8,128)S(1)}, s32[4,8,128]{2,1,0:T(8,128)}, u32[]{:S(2)}) %copy-start.5) | copy-done | bytes 16408
  5.7 27.6 %deposit_filter_drag.1 = (f32[5,4,8,128]{3,2,1,0:T(8,128)S(1)}, f32[3,4,4,8,128]{4,3,2,1,0:T(8,128)S(1)}) custom-call(s32[4,8,128]{2,1,0:T(8,128)S(1)} %copy-done.5, f32[3,4,4,8,128]{4,3,2,1,0:T(8,128)S(1)} %copy-done, f32[4,4,8,128]{3,2,1,0:T(8,128)S(1)} %copy-done.2, f32[4,4,8,128]{3,2,1,0:T(8,128)S(1)} %copy-done.3, f32[3,4,4,8,128]{4,3,2,1,0:T(8,128)S(1)} %copy-done.1, ...), custom_call_target="tpu_custom_call" | custom-call | tf_op jit(solution)/shard_map/deposit_filter_drag/pallas_call | solution.py:402
  33.3 0.6 %copy.10 = f32[5,4,8,128]{3,2,1,0:T(8,128)} copy(f32[5,4,8,128]{3,2,1,0:T(8,128)S(1)} %get-tuple-element.4) | data formatting | bytes 163840
  33.9 0.7 %copy.11 = f32[3,4,4,8,128]{4,3,2,1,0:T(8,128)} copy(f32[3,4,4,8,128]{4,3,2,1,0:T(8,128)S(1)} %get-tuple-element.5) | data formatting | bytes 393216
Async XLA Ops:
  0.6 0.9 %copy-start = (f32[3,4,4,8,128]{4,3,2,1,0:T(8,128)S(1)}, f32[3,4,4,8,128]{4,3,2,1,0:T(8,128)}, u32[]{:S(2)}) copy-start(f32[3,4,4,8,128]{4,3,2,1,0:T(8,128)} %offsets_h.1) | copy-start | bytes 589828
  1.6 0.9 %copy-start.1 = (f32[3,4,4,8,128]{4,3,2,1,0:T(8,128)S(1)}, f32[3,4,4,8,128]{4,3,2,1,0:T(8,128)}, u32[]{:S(2)}) copy-start(f32[3,4,4,8,128]{4,3,2,1,0:T(8,128)} %pv_h.1) | copy-start | bytes 589828
  2.5 0.8 %copy-start.2 = (f32[4,4,8,128]{3,2,1,0:T(8,128)S(1)}, f32[4,4,8,128]{3,2,1,0:T(8,128)}, u32[]{:S(2)}) copy-start(f32[4,4,8,128]{3,2,1,0:T(8,128)} %volume_h.1) | copy-start | bytes 196612
  3.3 0.8 %copy-start.3 = (f32[4,4,8,128]{3,2,1,0:T(8,128)S(1)}, f32[4,4,8,128]{3,2,1,0:T(8,128)}, u32[]{:S(2)}) copy-start(f32[4,4,8,128]{3,2,1,0:T(8,128)} %beta_h.1) | copy-start | bytes 196612
  4.2 0.8 %copy-start.4 = (f32[3,4,8,128]{3,2,1,0:T(8,128)S(1)}, f32[3,4,8,128]{3,2,1,0:T(8,128)}, u32[]{:S(2)}) copy-start(f32[3,4,8,128]{3,2,1,0:T(8,128)} %gas_h.1) | copy-start | bytes 147460
  5.0 0.7 %copy-start.5 = (s32[4,8,128]{2,1,0:T(8,128)S(1)}, s32[4,8,128]{2,1,0:T(8,128)}, u32[]{:S(2)}) copy-start(s32[4,8,128]{2,1,0:T(8,128)} %counts_h.1) | copy-start | bytes 49156

commit v2 on v1

--- a/solution.py
+++ b/solution.py
@@ -3,6 +3,7 @@
 
 import jax
 import jax.numpy as jnp
+import numpy as np
 from jax import lax
 from jax.experimental import pallas as pl
 from jax.experimental.pallas import tpu as pltpu
@@ -13,12 +14,27 @@
 SIGMA = 0.6
 INV_S2 = 1.0 / (SIGMA * SIGMA)
 CENTRE = math.exp(0.5 * INV_S2)
+ITERS = 4
+FILTER = 2.0
 
 DIAG = ((-1, -1), (-1, 1), (1, -1), (1, 1))
 ALL = ([(0, a, b) for a in (-1, 0, 1) for b in (-1, 0, 1) if (a, b) != (0, 0)]
        + [(-1, 0, 0), (1, 0, 0), (-2, 0, 0), (2, 0, 0)])
 
 
+def filter_taps():
+    unit = np.zeros((2 * ITERS + 3,) * 3)
+    unit[(ITERS + 1,) * 3] = 1.0
+    current = unit
+    for _ in range(ITERS):
+        around = sum(np.roll(current, step, axis) for axis in range(3) for step in (-1, 1))
+        current = (unit + FILTER * around) / (1.0 + 6.0 * FILTER)
+    return current[ITERS + 1:, ITERS + 1:, ITERS + 1:]
+
+
+TAPS = filter_taps()
+
+
 def rot(value, shift, axis):
     size = value.shape[axis]
     return pltpu.roll(value, shift % size, axis)
@@ -26,7 +42,7 @@
 
 def kernel(sizes, counts_h, offsets_h, volume_h, beta_h, pv_h, gas_h, filtered_h, drag_h,
            counts_v, offsets_v, src_v, pv_v, gas_v, occ_v, prod_v, shifted_v,
-           dm_v, dy_v, dz_v, dyz_v, mx_v, mxy_v,
+           dm_v, dy_v, dz_v, dyz_v,
            sy_v, sz_v, sd_v, ry_v, rz_v, rd_v,
            sgy_v, sgz_v, rgy_v, rgz_v, rgd_v,
            fx_v, fx2_v, rx_v, rx2_v, out_v, drag_v,
@@ -110,23 +126,32 @@
     lane0, lane127, col_low = lane == 0, lane == 127, col < 4
     col3, col4 = col == 3, col == 4
 
-    coef = F32(2.0 / 13.0)
-    plane = lax.broadcasted_iota(jnp.int32, (14, 8, 128), 0) + (4 * me[0] - 5)
-    in_x = jnp.where((plane >= 0) & (plane < 4 * sizes[0]), coef, 0.0)
-    row_ok = jnp.where(row_low, (me[1] < sizes[1] - 1).astype(F32), (me[1] > 0).astype(F32))
-    mx_v[...] = in_x
-    mxy_v[...] = in_x * row_ok[None]
-    slot_plane = slot + (4 * me[0] - 5)
-    cz = jnp.where((slot_plane >= 0) & (slot_plane < 4 * sizes[0]), coef, 0.0) * jnp.where(
-        col_low, (me[2] > 0).astype(F32), (me[2] < sizes[2] - 1).astype(F32))
-    cyz = cz * row_ok
-
+    edge_rows = (row_low & (me[1] == sizes[1] - 1)) | (~row_low & (me[1] == 0))
+    edge_cols = (col_low & (me[2] == 0)) | (~col_low & (me[2] == sizes[2] - 1))
+    keep_first, keep_last = (me[0] > 0).astype(F32), (me[0] < sizes[0] - 1).astype(F32)
+
+    def mirror_rows(tiles, spill):
+        image = jnp.where((row == 1) | (row == 4), rot(tiles, 2, tiles.ndim - 2), jnp.where(
+            (row == 2) | (row == 5), rot(tiles, 4, tiles.ndim - 2),
+            jnp.where((row == 3) | (row == 6), rot(tiles, 6, tiles.ndim - 2), 0.0)))
+        return jnp.where(edge_rows, -image, spill)
+
+    def mirror_cols(packed, spill):
+        image = jnp.where(col == 0, rot(packed, -6, 1), jnp.where(col == 1, rot(packed, -4, 1), jnp.where(
+            col == 2, rot(packed, -2, 1), jnp.where(col == 5, rot(packed, 2, 1), jnp.where(
+                col == 6, rot(packed, 4, 1), jnp.where(col == 7, rot(packed, 6, 1), 0.0))))))
+        return jnp.where(edge_cols, -image, spill)
+
+    enters_last = (me[0] == 0) & (me[1] == 0) & (me[2] == 0)
     loads[0].wait()
-    pl.semaphore_wait(barrier, greeted)
     gas_x = [((-1, 0, 0), gas_v.at[:, 1], gas_v.at[:, 5], gx_ss.at[0], gx_rs.at[1]),
              ((1, 0, 0), gas_v.at[:, 4], gas_v.at[:, 0], gx_ss.at[1], gx_rs.at[0])]
-    for item in gas_x:
-        send(*item)
+
+    @pl.when(enters_last)
+    def _():
+        pl.semaphore_wait(barrier, greeted)
+        for item in gas_x:
+            send(*item)
 
     loads[1].wait()
     loads[2].wait()
@@ -170,10 +195,10 @@
 
     def deposit(k, carry):
         src = [src_v[k, s] for s in range(4)]
-        mz, zz = [], []
-        for b in range(3):
-            by_z = []
-            for c in range(3):
+        by_z = []
+        for c in range(3):
+            by_y = []
+            for b in range(3):
                 by_x = []
                 for a in range(3):
                     total = src[0] * prod_v[9 * a + 3 * b + c, 0]
@@ -181,29 +206,30 @@
                         total = total + src[s] * prod_v[9 * a + 3 * b + c, s]
                     by_x.append(total)
                 lo, mid, hi = by_x
-                by_z.append(jnp.concatenate([
+                by_y.append(jnp.concatenate([
                     lo[0:1], lo[1:2] + mid[0:1], lo[2:4] + mid[1:3] + hi[0:2], mid[3:4] + hi[2:3], hi[3:4]], axis=0))
-            up, down = rot(by_z[2], 1, 2), rot(by_z[0], -1, 2)
-            mz.append(by_z[1] + jnp.where(lane0[None], 0.0, up) + jnp.where(lane127[None], 0.0, down))
-            spill = jnp.where(lane0[None], up, jnp.where(lane127[None], down, 0.0))
-            packed = rot(spill[0], 36, 1)
-            for i in range(1, 6):
+            up, down = rot(by_y[2], 1, 1), rot(by_y[0], -1, 1)
+            by_z.append((by_y[1] + jnp.where(row0, 0.0, up) + jnp.where(row7, 0.0, down),
+                         jnp.where(row0, up, jnp.where(row7, down, 0.0))))
+        main, packs = [], []
+        for kind in range(2):
+            up, down = rot(by_z[2][kind], 1, 2), rot(by_z[0][kind], -1, 2)
+            spill = jnp.where(lane0, up, jnp.where(lane127, down, 0.0))
+            main.append(by_z[1][kind] + jnp.where(lane0, 0.0, up) + jnp.where(lane127, 0.0, down))
+            packed = rot(spill[0], 36, 1) * keep_first
+            for i in range(1, 5):
                 packed = packed + rot(spill[i], 8 * i + 36, 1)
-            zz.append(packed)
-        up, down = rot(mz[2], 1, 1), rot(mz[0], -1, 1)
-        m = mz[1] + jnp.where(row0[None], 0.0, up) + jnp.where(row7[None], 0.0, down)
-        y = jnp.where(row0[None], up, jnp.where(row7[None], down, 0.0))
-        up, down = rot(zz[2], 1, 0), rot(zz[0], -1, 0)
-        z = zz[1] + jnp.where(row0, 0.0, up) + jnp.where(row7, 0.0, down)
-        yz = jnp.where(row0, up, jnp.where(row7, down, 0.0))
+            packs.append(packed + rot(spill[5], 76, 1) * keep_last)
+        m, y = [jnp.concatenate([v[0:1] * keep_first, v[1:5], v[5:6] * keep_last], axis=0) for v in main]
+        z, yz = packs
+        y, yz = mirror_rows(m, y), mirror_rows(z, yz)
+        mp, yp = pack(m, 4), pack(y, 4)
+        z, yz = mirror_cols(mp, z), mirror_cols(yp, yz)
         dm_v[k], dy_v[k], dz_v[k], dyz_v[k] = m, y, z, yz
-        sy_v[0, k, 0:6] = jnp.where(row_low[None], m, y)
-        sy_v[1, k, 0:6] = jnp.where(row_low[None], y, m)
+        sy_v[0, k, 0:6] = jnp.where(row_low, m, y)
+        sy_v[1, k, 0:6] = jnp.where(row_low, y, m)
         sy_v[0, k, 6] = jnp.where(row_low, z, yz)
         sy_v[1, k, 6] = jnp.where(row_low, yz, z)
-        for n in range(2):
-            send(*y_copy(n, k))
-        mp, yp = pack(m, 4), pack(y, 4)
         zm = (jnp.where(col_low, z, mp), jnp.where(col_low, mp, z))
         zy = (jnp.where(col_low, yz, yp), jnp.where(col_low, yp, yz))
         for n in range(2):
@@ -214,6 +240,19 @@
         return carry
 
     lax.fori_loop(0, 5, deposit, 0)
+
+    @pl.when(jnp.logical_not(enters_last))
+    def _():
+        pl.semaphore_wait(barrier, greeted)
+        for item in gas_x:
+            send(*item)
+
+    def send_y(k, carry):
+        for n in range(2):
+            send(*y_copy(n, k))
+        return carry
+
+    lax.fori_loop(0, 5, send_y, 0)
     z_copies = [((0, 0, s), sz_v.at[n], rz_v.at[1 - n], z_ss.at[n], z_rs.at[1 - n]) for n, s in enumerate((-1, 1))]
     d_copies = [((0, a, b), sd_v.at[n], rd_v.at[3 - n], d_ss.at[n], d_rs.at[3 - n]) for n, (a, b) in enumerate(DIAG)]
     for item in d_copies + z_copies:
@@ -244,31 +283,6 @@
                 ((1, 0, 0), fx_v.at[1, k], rx_v.at[0, k], x_ss.at[1, k], x_rs.at[0, k]),
                 ((-2, 0, 0), fx2_v.at[0, k], rx2_v.at[1, k], x2_ss.at[0, k], x2_rs.at[1, k]),
                 ((2, 0, 0), fx2_v.at[1, k], rx2_v.at[0, k], x2_ss.at[1, k], x2_rs.at[0, k])]
-
-    def widen(cur):
-        count = cur.shape[0]
-        return jnp.concatenate([cur[0:1], cur[1:2], cur[0:count - 2] + cur[2:count],
-                                cur[count - 2:count - 1], cur[count - 1:count]], axis=0)
-
-    def z_sum(tiles, halo, first):
-        edge = unpack(halo, first, tiles.shape[0])
-        return (rot(jnp.where(lane0[None], edge, tiles), -1, 2) + rot(jnp.where(lane127[None], edge, tiles), 1, 2))
-
-    def y_sum(tiles, halo):
-        axis = tiles.ndim - 2
-        return rot(jnp.where(row0, halo, tiles), -1, axis) + rot(jnp.where(row7, halo, tiles), 1, axis)
-
-    def packed_sum(tile, edges):
-        return (rot(tile, 8, 1) + rot(tile, -8, 1) + rot(jnp.where(col4, edges, tile), -1, 1)
-                + rot(jnp.where(col3, edges, tile), 1, 1))
-
-    def grow(total, inner):
-        count = total.shape[0]
-        return jnp.concatenate([total[0:1], total[1:count - 1] + inner, total[count - 1:count]], axis=0)
-
-    def add_source(total, source, lead):
-        count = total.shape[0]
-        return jnp.concatenate([total[0:lead], total[lead:lead + 6] + source, total[lead + 6:count]], axis=0)
 
     def filter_one(k, carry):
         for n in range(2):
@@ -288,32 +302,45 @@
         ends = (lane0 | lane127)[None]
         m = m + jnp.where(ends, unpack(jnp.where(col_low, side[1][0], side[0][0]), 4, 6), 0.0)
         y = y + jnp.where(ends, unpack(jnp.where(col_low, side[1][1], side[0][1]), 4, 6), 0.0)
-        m13, y13 = m * (0.5 * mx_v[4:10]), y * (0.5 * mxy_v[4:10])
-        z13, yz13 = z * (0.5 * cz), yz * (0.5 * cyz)
-        cm, cy, cz_now, cyz_now = m13, y13, z13, yz13
-        for sweep in range(1, 5):
-            first = 5 - sweep
-            gain = F32(13.0) if sweep == 1 else None
-            scale_m = mx_v[first - 1:first + 5 + 2 * sweep]
-            m_sum = grow(widen(cm), y_sum(cm, cy) + z_sum(cm, cz_now, first))
-            if gain is not None:
-                m_sum = m_sum * gain
-            next_m = add_source(m_sum * scale_m, m13, sweep)
-            if sweep < 4:
-                scale_y = mxy_v[first - 1:first + 5 + 2 * sweep]
-                y_total = grow(widen(cy), y_sum(cy, cm) + z_sum(cy, cyz_now, first))
-                z_total = packed_sum(cz_now, pack(cm, first)) + y_sum(cz_now, cyz_now)
-                yz_total = packed_sum(cyz_now, pack(cy, first)) + y_sum(cyz_now, cz_now)
-                if gain is not None:
-                    y_total, z_total, yz_total = y_total * gain, z_total * gain, yz_total * gain
-                cy = add_source(y_total * scale_y, y13, sweep)
-                cz_now, cyz_now = z13 + z_total * cz, yz13 + yz_total * cyz
-            cm = next_m
-        fx2_v[0, k] = cm[0]
-        fx_v[0, k] = cm[1:5]
-        out_v[k] = cm[5:9]
-        fx_v[1, k] = cm[9:13]
-        fx2_v[1, k] = cm[13]
+        edge_m, edge_y = unpack(z, 4, 6), unpack(yz, 4, 6)
+        pushed = [None] * 14
+        for i in range(6):
+            parts = [None] * 5
+
+            def add(sum_s, sum_c, value):
+                for d in range(5 - sum_s - sum_c):
+                    term = value * F32(TAPS[d, sum_s, sum_c])
+                    parts[d] = term if parts[d] is None else parts[d] + term
+
+            for c in range(5):
+                rows = []
+                for kind, (tile, edge) in enumerate(((m[i], edge_m[i]), (y[i], edge_y[i]))):
+                    if c and not (kind and c == 4):
+                        tile = (rot(jnp.where(lane < c, edge, tile), -c, 1)
+                                + rot(jnp.where(lane >= 128 - c, edge, tile), c, 1))
+                    rows.append(tile)
+                add(0, c, rows[0])
+                for s in range(1, 5 - c):
+                    add(s, c, rot(jnp.where(row < s, rows[1], rows[0]), -s, 0)
+                        + rot(jnp.where(row >= 8 - s, rows[1], rows[0]), s, 0))
+            for d in range(5):
+                for q in {i + 4 - d, i + 4 + d}:
+                    pushed[q] = parts[d] if pushed[q] is None else pushed[q] + parts[d]
+        for n, target in enumerate((fx_v.at[0, k], out_v.at[k], fx_v.at[1, k])):
+            for i in range(4):
+                target[i] = pushed[1 + 4 * n + i]
+        fx2_v[0, k] = pushed[0]
+        fx2_v[1, k] = pushed[13]
+
+        @pl.when(me[0] == 0)
+        def _():
+            for i in range(3):
+                rx_v[0, k, i] = -pushed[3 - i]
+
+        @pl.when(me[0] == sizes[0] - 1)
+        def _():
+            for i in range(1, 4):
+                rx_v[1, k, i] = -pushed[13 - i]
         for item in x_copies(k):
             send(*item)
         return carry
@@ -407,7 +434,7 @@
             scratch_shapes=[
                 pltpu.VMEM((4, 8, 128), jnp.int32), vmem(3, 4, 4), vmem(5, 4, 4), vmem(3, 4, 4), vmem(3, 6),
                 vmem(4, 4), vmem(27, 4, 4), vmem(3, 9, 6),
-                vmem(5, 6), vmem(5, 6), vmem(5), vmem(5), vmem(14), vmem(14),
+                vmem(5, 6), vmem(5, 6), vmem(5), vmem(5),
                 vmem(2, 5, 7), vmem(2, 5, 2), vmem(4, 5), vmem(2, 5, 7), vmem(2, 5, 2), vmem(4, 5),
                 vmem(2, 3), vmem(3), vmem(2, 3), vmem(2, 3), vmem(4, 3),
                 vmem(2, 5, 4), vmem(2, 5), vmem(2, 5, 4), vmem(2, 5), vmem(5, 4), vmem(3, 4, 4),
@@ -418,7 +445,8 @@
             compiler_params=pltpu.CompilerParams(
                 collective_id=0, has_side_effects=True, vmem_limit_bytes=32 * 2**20),
             name="deposit_filter_drag",
-        )(counts, offsets, volume, beta, particle_velocity, gas_velocity)
+        )(*[pltpu.with_memory_space_constraint(v, pltpu.HBM) for v in (
+            counts, offsets, volume, beta, particle_velocity, gas_velocity)])
 
     in_specs = (
         P("gx", "gy", "gz"),

time: 35 us -> 25.8 us (0.74)
  the two profiles are of different devices: /device:TPU:1 before, /device:TPU:2 now
where the time goes in v2:
time: 25.8 us; the launch traced here: 25.6 us
  Pallas kernels  23.7 us (92%)
  local copies, waits for them, and re-layouts  1.31 us (5%)
  between operations  0.64 us (2%)
    pallas_call x1, Pallas kernels, shards(): pl.pallas_call(functools.partial(kernel, sizes), out_shape=(jax.ShapeDtyp...  23.7 us
    unnamed x2, local copies, waits for them, and re-layouts  1.31 us

profile of v2, /device:TPU:2, one launch (start us, length us, event | category | flops | bytes accessed | tf_op | source)
XLA Modules:
  0.0 25.6 jit_solution(9927097131628648080)
XLA Ops:
  0.6 23.7 %deposit_filter_drag.1 = (f32[5,4,8,128]{3,2,1,0:T(8,128)S(1)}, f32[3,4,4,8,128]{4,3,2,1,0:T(8,128)S(1)}) custom-call(s32[4,8,128]{2,1,0:T(8,128)} %counts_h.1, f32[3,4,4,8,128]{4,3,2,1,0:T(8,128)} %offsets_h.1, f32[4,4,8,128]{3,2,1,0:T(8,128)} %volume_h.1, f32[4,4,8,128]{3,2,1,0:T(8,128)} %beta_h.1, f32[3,4,4,8,128]{4,3,2,1,0:T(8,128)} %pv_h.1, ...), custom_call_target="tpu_custom_call" | custom-call | tf_op jit(solution)/shard_map/deposit_filter_drag/pallas_call | solution.py:429
  24.3 0.6 %copy.10 = f32[5,4,8,128]{3,2,1,0:T(8,128)} copy(f32[5,4,8,128]{3,2,1,0:T(8,128)S(1)} %get-tuple-element.4) | data formatting | bytes 163840
  25.0 0.7 %copy.11 = f32[3,4,4,8,128]{4,3,2,1,0:T(8,128)} copy(f32[3,4,4,8,128]{4,3,2,1,0:T(8,128)S(1)} %get-tuple-element.5) | data formatting | bytes 393216

commit v3 on v2

v3 whole, which is shorter than its diff:
```python
import functools
import math

import jax
import jax.numpy as jnp
import numpy as np
from jax import lax
from jax.experimental import pallas as pl
from jax.experimental.pallas import tpu as pltpu
from jax.sharding import PartitionSpec as P

MESH = pl.DeviceIdType.MESH
F32 = jnp.float32
SIGMA = 0.6
INV_S2 = 1.0 / (SIGMA * SIGMA)
CENTRE = math.exp(0.5 * INV_S2)
ITERS = 4
FILTER = 2.0

GROUPS = ((0, 2), (2, 4), (4, 5))
DIAG = ((-1, -1), (-1, 1), (1, -1), (1, 1))
ALL = ([(0, a, b) for a in (-1, 0, 1) for b in (-1, 0, 1) if (a, b) != (0, 0)]
       + [(-1, 0, 0), (1, 0, 0), (-2, 0, 0), (2, 0, 0)])


def filter_taps():
    unit = np.zeros((2 * ITERS + 3,) * 3)
    unit[(ITERS + 1,) * 3] = 1.0
    current = unit
    for _ in range(ITERS):
        around = sum(np.roll(current, step, axis) for axis in range(3) for step in (-1, 1))
        current = (unit + FILTER * around) / (1.0 + 6.0 * FILTER)
    return current[ITERS + 1:, ITERS + 1:, ITERS + 1:]


TAPS = filter_taps()


def rot(value, shift, axis):
    size = value.shape[axis]
    return pltpu.roll(value, shift % size, axis)


def kernel(sizes, counts_h, offsets_h, volume_h, beta_h, pv_h, gas_h, filtered_o, drag_o,
           counts_v, offsets_v, src_v, pv_v, gas_v, occ_v, prod_v, shifted_v, dm_v, dy_v, dz_v, dyz_v,
           sy_v, sz_v, sd_v, sx_v, sx2_v, ry_v, rz_v, rd_v, rx_v, rx2_v, sgz_v,
           in_sem, y_ss, z_ss, d_ss, x_ss, x2_ss, y_rs, z_rs, d_rs, gx_rs, x_rs, x2_rs, late_sem):
    me = (lax.axis_index("gx"), lax.axis_index("gy"), lax.axis_index("gz"))

    def near(step):
        place = tuple(me[i] + step[i] for i in range(3))
        ok = None
        for i in range(3):
            if step[i]:
                inside = place[i] >= 0 if step[i] < 0 else place[i] < sizes[i]
                ok = inside if ok is None else ok & inside
        origin = None
        if max(step) <= 0:
            origin = (place[0] == 0) & (place[1] == 0) & (place[2] == 0)
        return place, ok, origin

    def copy(step, src, dst, ssem, rsem):
        return pltpu.make_async_remote_copy(src_ref=src, dst_ref=dst, send_sem=ssem, recv_sem=rsem,
                                            device_id=near(step)[0], device_id_type=MESH)

    def send(items, to_origin=None):
        _, ok, origin = near(items[0][0])
        if to_origin is not None and origin is not None:
            ok = origin if to_origin else ok & jnp.logical_not(origin)
        elif to_origin:
            return

        @pl.when(ok)
        def _():
            for item in items:
                copy(*item).start()

    def wait_recv(step, dst, rsem):
        @pl.when(near(step)[1])
        def _():
            copy(step, dst, dst, rsem, rsem).wait_recv()

    def wait_send(step, src, ssem):
        @pl.when(near(step)[1])
        def _():
            copy(step, src, src, ssem, ssem).wait_send()

    loads = [
        pltpu.make_async_copy(offsets_h, offsets_v, in_sem.at[0]),
        pltpu.make_async_copy(counts_h, counts_v, in_sem.at[1]),
        pltpu.make_async_copy(gas_h, gas_v.at[:, pl.ds(1, 4)], in_sem.at[2]),
        pltpu.make_async_copy(volume_h, src_v.at[0], in_sem.at[3]),
        pltpu.make_async_copy(beta_h, src_v.at[1], in_sem.at[4]),
        pltpu.make_async_copy(pv_h, pv_v, in_sem.at[5]),
    ]
    for load in loads:
        load.start()

    is_origin = (me[0] == 0) & (me[1] == 0) & (me[2] == 0)
    barrier = pltpu.get_barrier_semaphore()
    greeted = jnp.int32(0)
    for step in ALL:
        place, ok, origin = near(step)
        greets = ok if origin is None else ok & jnp.logical_not(origin)
        greeted = greeted + greets.astype(jnp.int32)

        @pl.when(ok & jnp.logical_not(is_origin))
        def _():
            pl.semaphore_signal(barrier, inc=1, device_id=place, device_id_type=MESH)

    @pl.when(is_origin)
    def _():
        pl.semaphore_wait(barrier, greeted)
        for step in ALL:
            if min(step) >= 0:
                place, ok, _ = near(step)

                @pl.when(ok)
                def _():
                    pl.semaphore_signal(late_sem, inc=1, device_id=place, device_id_type=MESH)

    def clear(step, refs):
        @pl.when(jnp.logical_not(near(step)[1]))
        def _():
            for ref in refs:
                ref[...] = jnp.zeros(ref.shape, F32)

    for n, s in enumerate((-1, 1)):
        clear((s, 0, 0), [rx_v.at[n]])
        clear((2 * s, 0, 0), [rx2_v.at[n]])
        clear((0, s, 0), [ry_v.at[n]])
        clear((0, 0, s), [rz_v.at[n]])
    for n, (a, b) in enumerate(DIAG):
        clear((0, a, b), [rd_v.at[n]])

    row = lax.broadcasted_iota(jnp.int32, (8, 128), 0)
    lane = lax.broadcasted_iota(jnp.int32, (8, 128), 1)
    slot, col = lane >> 3, lane & 7
    row0, row7, row_low = row == 0, row == 7, row < 4
    lane0, lane127, col_low = lane == 0, lane == 127, col < 4

    edge_rows = (row_low & (me[1] == sizes[1] - 1)) | (~row_low & (me[1] == 0))
    edge_cols = (col_low & (me[2] == 0)) | (~col_low & (me[2] == sizes[2] - 1))
    keep_first, keep_last = (me[0] > 0).astype(F32), (me[0] < sizes[0] - 1).astype(F32)

    def mirror_rows(tiles, spill):
        image = jnp.where((row == 1) | (row == 4), rot(tiles, 2, tiles.ndim - 2), jnp.where(
            (row == 2) | (row == 5), rot(tiles, 4, tiles.ndim - 2),
            jnp.where((row == 3) | (row == 6), rot(tiles, 6, tiles.ndim - 2), 0.0)))
        return jnp.where(edge_rows, -image, spill)

    def mirror_cols(packed, spill):
        image = jnp.where(col == 0, rot(packed, -6, 1), jnp.where(col == 1, rot(packed, -4, 1), jnp.where(
            col == 2, rot(packed, -2, 1), jnp.where(col == 5, rot(packed, 2, 1), jnp.where(
                col == 6, rot(packed, 4, 1), jnp.where(col == 7, rot(packed, 6, 1), 0.0))))))
        return jnp.where(edge_cols, -image, spill)

    def part(n, ref, per, g):
        first, last = GROUPS[g]
        return ref.at[n, pl.ds(per * first, per * (last - first))]

    def gas_x(n):
        return ((-1, 1)[n], 0, 0), sx_v.at[n, pl.ds(20, 3)], rx_v.at[1 - n, pl.ds(20, 3)], x_ss.at[n], gx_rs.at[1 - n]

    def send_gas_x(to_origin):
        for n in range(2):
            send([gas_x(n)], to_origin)

    def send_group(g, to_origin):
        for n, (a, b) in enumerate(DIAG):
            send([((0, a, b), part(n, sd_v, 1, g), part(3 - n, rd_v, 1, g), d_ss.at[n], d_rs.at[3 - n, g])], to_origin)
        for n in range(2):
            send([((0, 0, (-1, 1)[n]), part(n, sz_v, 2, g), part(1 - n, rz_v, 2, g), z_ss.at[n], z_rs.at[1 - n, g])],
                 to_origin)
            send([((0, (-1, 1)[n], 0), part(n, sy_v, 7, g), part(1 - n, ry_v, 7, g), y_ss.at[n], y_rs.at[1 - n, g])],
                 to_origin)

    def wait_group(g):
        for n in range(2):
            wait_recv((0, (-1, 1)[n], 0), part(n, ry_v, 7, g), y_rs.at[n, g])
            wait_recv((0, 0, (-1, 1)[n]), part(n, rz_v, 2, g), z_rs.at[n, g])
        for n, (a, b) in enumerate(DIAG):
            wait_recv((0, a, b), part(n, rd_v, 1, g), d_rs.at[n, g])

    loads[0].wait()
    loads[1].wait()

    def products(s, carry):
        occ = jnp.where(counts_v[...] > s, F32(1.0), F32(0.0))
        occ_v[s] = occ
        weights, norm = [], None
        for axis in range(3):
            t = jnp.exp((0.5 - offsets_v[axis, s]) * INV_S2)
            low, mid = t * t, CENTRE * t
            total = low + mid + 1.0
            norm = total if norm is None else norm * total
            weights.append((low, mid))
        scale = occ / norm
        wx = (weights[0][0] * scale, weights[0][1] * scale, scale)
        for a in range(3):
            for b in range(3):
                xy = wx[a] * weights[1][b] if b < 2 else wx[a]
                for c in range(3):
                    prod_v[9 * a + 3 * b + c, s] = xy * weights[2][c] if c < 2 else xy
        return carry

    lax.fori_loop(0, 4, products, 0, unroll=True)
    loads[2].wait()
    for j in range(3):
        sx_v[0, 20 + j] = gas_v[j, 1]
        sx_v[1, 20 + j] = gas_v[j, 4]

    @pl.when(is_origin)
    def _():
        send_gas_x(None)

    for load in loads[3:]:
        load.wait()
    for j in range(3):
        src_v[2 + j] = src_v[1] * pv_v[j]

    def pack(planes, first):
        result = jnp.zeros((8, 128), F32)
        for i in range(planes.shape[0]):
            result = jnp.where(slot == first + i, rot(planes[i], 8 * (first + i) + 4, 1), result)
        return result

    def unpack(tile, first, count):
        return jnp.stack([rot(tile, -(8 * (first + i) + 4), 1) for i in range(count)])

    def deposit(k, carry):
        src = [src_v[k, s] for s in range(4)]
        by_z = []
        for c in range(3):
            by_y = []
            for b in range(3):
                by_x = []
                for a in range(3):
                    total = src[0] * prod_v[9 * a + 3 * b + c, 0]
                    for s in range(1, 4):
                        total = total + src[s] * prod_v[9 * a + 3 * b + c, s]
                    by_x.append(total)
                lo, mid, hi = by_x
                by_y.append(jnp.concatenate([
                    lo[0:1], lo[1:2] + mid[0:1], lo[2:4] + mid[1:3] + hi[0:2], mid[3:4] + hi[2:3], hi[3:4]], axis=0))
            up, down = rot(by_y[2], 1, 1), rot(by_y[0], -1, 1)
            by_z.append((by_y[1] + jnp.where(row0, 0.0, up) + jnp.where(row7, 0.0, down),
                         jnp.where(row0, up, jnp.where(row7, down, 0.0))))
        main, packs = [], []
        for kind in range(2):
            up, down = rot(by_z[2][kind], 1, 2), rot(by_z[0][kind], -1, 2)
            spill = jnp.where(lane0, up, jnp.where(lane127, down, 0.0))
            main.append(by_z[1][kind] + jnp.where(lane0, 0.0, up) + jnp.where(lane127, 0.0, down))
            packed = rot(spill[0], 36, 1) * keep_first
            for i in range(1, 5):
                packed = packed + rot(spill[i], 8 * i + 36, 1)
            packs.append(packed + rot(spill[5], 76, 1) * keep_last)
        m, y = [jnp.concatenate([v[0:1] * keep_first, v[1:5], v[5:6] * keep_last], axis=0) for v in main]
        z, yz = packs
        y, yz = mirror_rows(m, y), mirror_rows(z, yz)
        mp, yp = pack(m, 4), pack(y, 4)
        z, yz = mirror_cols(mp, z), mirror_cols(yp, yz)
        dm_v[k], dy_v[k], dz_v[k], dyz_v[k] = m, y, z, yz
        sy_v[0, pl.ds(7 * k, 6)] = jnp.where(row_low, m, y)
        sy_v[1, pl.ds(7 * k, 6)] = jnp.where(row_low, y, m)
        sy_v[0, 7 * k + 6] = jnp.where(row_low, z, yz)
        sy_v[1, 7 * k + 6] = jnp.where(row_low, yz, z)
        zm = (jnp.where(col_low, z, mp), jnp.where(col_low, mp, z))
        zy = (jnp.where(col_low, yz, yp), jnp.where(col_low, yp, yz))
        for n in range(2):
            sz_v[n, 2 * k], sz_v[n, 2 * k + 1] = zm[n], zy[n]
        for n, (a, b) in enumerate(DIAG):
            first, second = (zm, zy) if a < 0 else (zy, zm)
            sd_v[n, k] = jnp.where(row_low, first[(b + 1) // 2], second[(b + 1) // 2])
        return carry

    for g in range(3):
        lax.fori_loop(*GROUPS[g], deposit, 0, unroll=True)

        @pl.when(is_origin)
        def _():
            send_group(g, None)

    @pl.when(jnp.logical_not(is_origin))
    def _():
        pl.semaphore_wait(barrier, greeted)
        send_gas_x(False)
        for g in range(3):
            send_group(g, False)

    by_origin = jnp.bool_(False)
    for step in ALL:
        if max(step) <= 0:
            by_origin = by_origin | near(step)[2]

    @pl.when(by_origin)
    def _():
        pl.semaphore_wait(late_sem, 1)
        send_gas_x(True)
        for g in range(3):
            send_group(g, True)

    for n in range(2):
        wait_recv(((-1, 1)[n], 0, 0), rx_v.at[n, pl.ds(20, 3)], gx_rs.at[n])
    for j in range(3):
        gas_v[j, 0] = rx_v[0, 20 + j]
        gas_v[j, 5] = rx_v[1, 20 + j]
        sgz_v[j] = pack(gas_v[j], 4)
        for i in range(6):
            sy_v[0, 35 + j, pl.ds(i, 1), :] = gas_v[j, i, pl.ds(0, 1), :]
            sy_v[1, 35 + j, pl.ds(i, 1), :] = gas_v[j, i, pl.ds(7, 1), :]
        for n in range(2):
            sy_v[n, 35 + j, pl.ds(6, 2), :] = jnp.zeros((2, 128), F32)
    for n in range(2):
        send([((0, (-1, 1)[n], 0), sy_v.at[n, pl.ds(35, 3)], ry_v.at[1 - n, pl.ds(35, 3)], y_ss.at[n], y_rs.at[1 - n, 3])])
        send([((0, 0, (-1, 1)[n]), sgz_v, rz_v.at[1 - n, pl.ds(10, 3)], z_ss.at[n], z_rs.at[1 - n, 3])])
    for n, (a, b) in enumerate(DIAG):
        send([((0, a, b), sgz_v, rd_v.at[3 - n, pl.ds(5, 3)], d_ss.at[n], d_rs.at[3 - n, 3])])

    def filter_one(k, carry):
        below, above = ry_v[0, pl.ds(7 * k, 6)], ry_v[1, pl.ds(7 * k, 6)]
        below_z, above_z = ry_v[0, 7 * k + 6], ry_v[1, 7 * k + 6]
        m = dm_v[k] + jnp.where(row_low[None], below, above)
        y = dy_v[k] + jnp.where(row_low[None], above, below)
        side = []
        for n, b in enumerate((0, 1)):
            lower, upper = rd_v[b, k], rd_v[2 + b, k]
            side.append((rz_v[n, 2 * k] + jnp.where(row_low, lower, upper),
                         rz_v[n, 2 * k + 1] + jnp.where(row_low, upper, lower)))
        z = dz_v[k] + jnp.where(col_low, side[0][0], side[1][0]) + jnp.where(row_low, below_z, above_z)
        yz = dyz_v[k] + jnp.where(col_low, side[0][1], side[1][1]) + jnp.where(row_low, above_z, below_z)
        ends = (lane0 | lane127)[None]
        m = m + jnp.where(ends, unpack(jnp.where(col_low, side[1][0], side[0][0]), 4, 6), 0.0)
        y = y + jnp.where(ends, unpack(jnp.where(col_low, side[1][1], side[0][1]), 4, 6), 0.0)
        edge_m, edge_y = unpack(z, 4, 6), unpack(yz, 4, 6)
        pushed = [None] * 14
        for i in range(6):
            parts = [None] * 5

            def add(sum_s, sum_c, value):
                for d in range(5 - sum_s - sum_c):
                    term = value * F32(TAPS[d, sum_s, sum_c])
                    parts[d] = term if parts[d] is None else parts[d] + term

            for c in range(5):
                rows = []
                for kind, (tile, edge) in enumerate(((m[i], edge_m[i]), (y[i], edge_y[i]))):
                    if c and not (kind and c == 4):
                        tile = (rot(jnp.where(lane < c, edge, tile), -c, 1)
                                + rot(jnp.where(lane >= 128 - c, edge, tile), c, 1))
                    rows.append(tile)
                add(0, c, rows[0])
                for s in range(1, 5 - c):
                    add(s, c, rot(jnp.where(row < s, rows[1], rows[0]), -s, 0)
                        + rot(jnp.where(row >= 8 - s, rows[1], rows[0]), s, 0))
            for d in range(5):
                for q in {i + 4 - d, i + 4 + d}:
                    pushed[q] = parts[d] if pushed[q] is None else pushed[q] + parts[d]
        for i in range(4):
            sx_v[0, 4 * k + i] = pushed[1 + i]
            filtered_o[k, i] = pushed[5 + i]
            sx_v[1, 4 * k + i] = pushed[9 + i]
        sx2_v[0, k] = pushed[0]
        sx2_v[1, k] = pushed[13]

        @pl.when(me[0] == 0)
        def _():
            for i in range(3):
                rx_v[0, 4 * k + i] = -pushed[3 - i]

        @pl.when(me[0] == sizes[0] - 1)
        def _():
            for i in range(1, 4):
                rx_v[1, 4 * k + i] = -pushed[13 - i]
        return carry

    for g in range(3):
        wait_group(g)
        lax.fori_loop(*GROUPS[g], filter_one, 0, unroll=True)
        for n, s in enumerate((-1, 1)):
            send([((s, 0, 0), part(n, sx_v, 4, g), part(1 - n, rx_v, 4, g), x_ss.at[n], x_rs.at[1 - n])])
            send([((2 * s, 0, 0), part(n, sx2_v, 1, g), part(1 - n, rx2_v, 1, g), x2_ss.at[n], x2_rs.at[1 - n])])

    for n in range(2):
        wait_recv((0, (-1, 1)[n], 0), ry_v.at[n, pl.ds(35, 3)], y_rs.at[n, 3])
        wait_recv((0, 0, (-1, 1)[n]), rz_v.at[n, pl.ds(10, 3)], z_rs.at[n, 3])
    for n, (a, b) in enumerate(DIAG):
        wait_recv((0, a, b), rd_v.at[n, pl.ds(5, 3)], d_rs.at[n, 3])

    def shift(j, carry):
        tiles = gas_v[j]
        below, above = ry_v[0, 35 + j], ry_v[1, 35 + j]
        rows = jnp.stack([jnp.where(row0, jnp.broadcast_to(above[i:i + 1], (8, 128)),
                                    jnp.broadcast_to(below[i:i + 1], (8, 128))) for i in range(6)])
        halo_m = jnp.where(col_low, rz_v[0, 10 + j], rz_v[1, 10 + j])
        halo_y = jnp.where(col_low, jnp.where(row0, rd_v[2, 5 + j], rd_v[0, 5 + j]),
                           jnp.where(row0, rd_v[3, 5 + j], rd_v[1, 5 + j]))
        variants = []
        for value, halo in ((tiles, halo_m), (rows, halo_y)):
            edge = unpack(halo, 4, 6)
            variants.append((rot(jnp.where(lane127[None], edge, value), 1, 2), value,
                             rot(jnp.where(lane0[None], edge, value), -1, 2)))
        for c in range(3):
            value, halo = variants[0][c], variants[1][c]
            shifted_v[j, c] = rot(jnp.where(row7[None], halo, value), 1, 1)
            shifted_v[j, 3 + c] = value
            shifted_v[j, 6 + c] = rot(jnp.where(row0[None], halo, value), -1, 1)
        return carry

    lax.fori_loop(0, 3, shift, 0, unroll=True)

    def drag(x, carry):
        totals = [jnp.zeros((4, 8, 128), F32) for _ in range(3)]
        for a in range(3):
            for bc in range(9):
                weight = prod_v[9 * a + bc, :, x]
                for j in range(3):
                    totals[j] = totals[j] + weight * shifted_v[j, bc, x + a][None]
        for j in range(3):
            drag_o[j, :, x] = src_v[1, :, x] * totals[j] - occ_v[:, x] * src_v[2 + j, :, x]
        return carry

    lax.fori_loop(0, 4, drag, 0, unroll=True)

    for n, s in enumerate((-1, 1)):
        wait_recv((s, 0, 0), rx_v.at[n, pl.ds(0, 20)], x_rs.at[n])
        wait_recv((2 * s, 0, 0), rx2_v.at[n], x2_rs.at[n])
    for k in range(5):
        for i in range(4):
            total = filtered_o[k, i] + (rx_v[0, 4 * k + i] + rx_v[1, 4 * k + i])
            if i in (0, 3):
                total = total + rx2_v[i // 3, k]
            filtered_o[k, i] = total

    for n, s in enumerate((-1, 1)):
        wait_send((0, s, 0), sy_v.at[n], y_ss.at[n])
        wait_send((0, 0, s), sz_v.at[n], z_ss.at[n])
        wait_send((s, 0, 0), sx_v.at[n], x_ss.at[n])
        wait_send((2 * s, 0, 0), sx2_v.at[n], x2_ss.at[n])
    for n, (a, b) in enumerate(DIAG):
        wait_send((0, a, b), sd_v.at[n], d_ss.at[n])


def store(filtered_v, drag_v, filtered_h, drag_h, sem):
    copies = [pltpu.make_async_copy(filtered_v, filtered_h, sem.at[0]), pltpu.make_async_copy(drag_v, drag_h, sem.at[1])]
    for item in copies:
        item.start()
    for item in copies:
        item.wait()


def solution(mesh):
    sizes = tuple(mesh.shape[name] for name in ("gx", "gy", "gz"))
    dma = pltpu.SemaphoreType.DMA

    def vmem(*shape):
        return pltpu.VMEM(shape + (8, 128), F32)

    def shards(counts, offsets, volume, beta, particle_velocity, gas_velocity):
        any_space = pl.BlockSpec(memory_space=pl.ANY)
        out_shape = (jax.ShapeDtypeStruct((5, 4, 8, 128), F32), jax.ShapeDtypeStruct((3, 4, 4, 8, 128), F32))
        filtered, drag = pl.pallas_call(
            functools.partial(kernel, sizes),
            out_shape=out_shape,
            in_specs=[any_space] * 6,
            out_specs=(pl.BlockSpec(memory_space=pltpu.VMEM),) * 2,
            scratch_shapes=[
                pltpu.VMEM((4, 8, 128), jnp.int32), vmem(3, 4, 4), vmem(5, 4, 4), vmem(3, 4, 4), vmem(3, 6),
                vmem(4, 4), vmem(27, 4, 4), vmem(3, 9, 6), vmem(5, 6), vmem(5, 6), vmem(5), vmem(5),
                vmem(2, 38), vmem(2, 13), vmem(4, 8), vmem(2, 23), vmem(2, 5),
                vmem(2, 38), vmem(2, 13), vmem(4, 8), vmem(2, 23), vmem(2, 5), vmem(3),
                dma((6,)), dma((2,)), dma((2,)), dma((4,)), dma((2,)), dma((2,)),
                dma((2, 4)), dma((2, 4)), dma((4, 4)), dma((2,)), dma((2,)), dma((2,)), pltpu.SemaphoreType.REGULAR,
            ],
            compiler_params=pltpu.CompilerParams(
                collective_id=0, has_side_effects=True, vmem_limit_bytes=32 * 2**20),
            name="deposit_filter_drag",
        )(*[pltpu.with_memory_space_constraint(v, pltpu.HBM) for v in (
            counts, offsets, volume, beta, particle_velocity, gas_velocity)])
        return pl.pallas_call(
            store, out_shape=out_shape, in_specs=[any_space] * 2, out_specs=(any_space,) * 2,
            scratch_shapes=[dma((2,))], compiler_params=pltpu.CompilerParams(vmem_limit_bytes=2**20), name="store",
        )(filtered, drag)

    in_specs = (
        P("gx", "gy", "gz"),
        P(None, None, "gx", "gy", "gz"),
        P(None, "gx", "gy", "gz"),
        P(None, "gx", "gy", "gz"),
        P(None, None, "gx", "gy", "gz"),
        P(None, "gx", "gy", "gz"),
    )
    out_specs = (P(None, "gx", "gy", "gz"), P(None, None, "gx", "gy", "gz"))
    return jax.shard_map(shards, mesh=mesh, in_specs=in_specs, out_specs=out_specs, check_vma=False)
```

time: 25.8 us -> 23.6 us (0.915)
  the two profiles are of different devices: /device:TPU:2 before, /device:TPU:8 now
where the time goes in v3:
time: 23.6 us; the launch traced here: 23.4 us
  Pallas kernels  22.8 us (97%)
  between operations  0.64 us (3%)
    pallas_call x1, Pallas kernels, shards(): pl.pallas_call(functools.partial(kernel, sizes), out_shape=out_shape, in_...  22 us
    pallas_call x1, Pallas kernels, shards(): pl.pallas_call(store, out_shape=out_shape, in_specs=[any_space] * 2, out_...  0.72 us

profile of v3, /device:TPU:8, one launch (start us, length us, event | category | flops | bytes accessed | tf_op | source)
XLA Modules:
  0.0 23.4 jit_solution(13120492224273518806)
XLA Ops:
  0.6 22.0 %deposit_filter_drag.1 = (f32[5,4,8,128]{3,2,1,0:T(8,128)S(1)}, f32[3,4,4,8,128]{4,3,2,1,0:T(8,128)S(1)}) custom-call(s32[4,8,128]{2,1,0:T(8,128)} %counts_h.1, f32[3,4,4,8,128]{4,3,2,1,0:T(8,128)} %offsets_h.1, f32[4,4,8,128]{3,2,1,0:T(8,128)} %volume_h.1, f32[4,4,8,128]{3,2,1,0:T(8,128)} %beta_h.1, f32[3,4,4,8,128]{4,3,2,1,0:T(8,128)} %pv_h.1, ...), custom_call_target="tpu_custom_call" | custom-call | tf_op jit(solution)/shard_map/deposit_filter_drag/pallas_call | solution.py:462
  22.7 0.7 %store.1 = (f32[5,4,8,128]{3,2,1,0:T(8,128)}, f32[3,4,4,8,128]{4,3,2,1,0:T(8,128)}) custom-call(f32[5,4,8,128]{3,2,1,0:T(8,128)S(1)} %get-tuple-element.4.filtered_v, f32[3,4,4,8,128]{4,3,2,1,0:T(8,128)S(1)} %get-tuple-element.5.drag_v), custom_call_target="tpu_custom_call" | custom-call | tf_op jit(solution)/shard_map/store/pallas_call | solution.py:480

commit v4 on v3

--- a/solution.py
+++ b/solution.py
@@ -85,6 +85,16 @@
         def _():
             copy(step, src, src, ssem, ssem).wait_send()
 
+    is_origin = (me[0] == 0) & (me[1] == 0) & (me[2] == 0)
+    barrier = pltpu.get_barrier_semaphore()
+    late = [step for step in ALL if min(step) >= 0 and all(s < n for s, n in zip(step, sizes))]
+
+    @pl.when(is_origin)
+    def _():
+        pl.semaphore_wait(barrier, len(late))
+        for step in late:
+            pl.semaphore_signal(late_sem, inc=1, device_id=step, device_id_type=MESH)
+
     loads = [
         pltpu.make_async_copy(offsets_h, offsets_v, in_sem.at[0]),
         pltpu.make_async_copy(counts_h, counts_v, in_sem.at[1]),
@@ -96,28 +106,20 @@
     for load in loads:
         load.start()
 
-    is_origin = (me[0] == 0) & (me[1] == 0) & (me[2] == 0)
-    barrier = pltpu.get_barrier_semaphore()
     greeted = jnp.int32(0)
     for step in ALL:
-        place, ok, origin = near(step)
+        _, ok, origin = near(step)
         greets = ok if origin is None else ok & jnp.logical_not(origin)
         greeted = greeted + greets.astype(jnp.int32)
 
-        @pl.when(ok & jnp.logical_not(is_origin))
-        def _():
-            pl.semaphore_signal(barrier, inc=1, device_id=place, device_id_type=MESH)
-
-    @pl.when(is_origin)
+    @pl.when(jnp.logical_not(is_origin))
     def _():
-        pl.semaphore_wait(barrier, greeted)
         for step in ALL:
-            if min(step) >= 0:
-                place, ok, _ = near(step)
-
-                @pl.when(ok)
-                def _():
-                    pl.semaphore_signal(late_sem, inc=1, device_id=place, device_id_type=MESH)
+            place, ok, _ = near(step)
+
+            @pl.when(ok)
+            def _():
+                pl.semaphore_signal(barrier, inc=1, device_id=place, device_id_type=MESH)
 
     def clear(step, refs):
         @pl.when(jnp.logical_not(near(step)[1]))
@@ -300,22 +302,26 @@
         for g in range(3):
             send_group(g, True)
 
-    for n in range(2):
-        wait_recv(((-1, 1)[n], 0, 0), rx_v.at[n, pl.ds(20, 3)], gx_rs.at[n])
-    for j in range(3):
-        gas_v[j, 0] = rx_v[0, 20 + j]
-        gas_v[j, 5] = rx_v[1, 20 + j]
-        sgz_v[j] = pack(gas_v[j], 4)
-        for i in range(6):
-            sy_v[0, 35 + j, pl.ds(i, 1), :] = gas_v[j, i, pl.ds(0, 1), :]
-            sy_v[1, 35 + j, pl.ds(i, 1), :] = gas_v[j, i, pl.ds(7, 1), :]
+    def spread_gas():
         for n in range(2):
-            sy_v[n, 35 + j, pl.ds(6, 2), :] = jnp.zeros((2, 128), F32)
-    for n in range(2):
-        send([((0, (-1, 1)[n], 0), sy_v.at[n, pl.ds(35, 3)], ry_v.at[1 - n, pl.ds(35, 3)], y_ss.at[n], y_rs.at[1 - n, 3])])
-        send([((0, 0, (-1, 1)[n]), sgz_v, rz_v.at[1 - n, pl.ds(10, 3)], z_ss.at[n], z_rs.at[1 - n, 3])])
-    for n, (a, b) in enumerate(DIAG):
-        send([((0, a, b), sgz_v, rd_v.at[3 - n, pl.ds(5, 3)], d_ss.at[n], d_rs.at[3 - n, 3])])
+            wait_recv(((-1, 1)[n], 0, 0), rx_v.at[n, pl.ds(20, 3)], gx_rs.at[n])
+        for j in range(3):
+            gas_v[j, 0] = rx_v[0, 20 + j]
+            gas_v[j, 5] = rx_v[1, 20 + j]
+            sgz_v[j] = pack(gas_v[j], 4)
+            for i in range(6):
+                sy_v[0, 35 + j, pl.ds(i, 1), :] = gas_v[j, i, pl.ds(0, 1), :]
+                sy_v[1, 35 + j, pl.ds(i, 1), :] = gas_v[j, i, pl.ds(7, 1), :]
+            for n in range(2):
+                sy_v[n, 35 + j, pl.ds(6, 2), :] = jnp.zeros((2, 128), F32)
+        for n in range(2):
+            send([((0, (-1, 1)[n], 0), sy_v.at[n, pl.ds(35, 3)], ry_v.at[1 - n, pl.ds(35, 3)], y_ss.at[n], y_rs.at[1 - n, 3])])
+            send([((0, 0, (-1, 1)[n]), sgz_v, rz_v.at[1 - n, pl.ds(10, 3)], z_ss.at[n], z_rs.at[1 - n, 3])])
+        for n, (a, b) in enumerate(DIAG):
+            send([((0, a, b), sgz_v, rd_v.at[3 - n, pl.ds(5, 3)], d_ss.at[n], d_rs.at[3 - n, 3])])
+
+    after_filter = (me[0] == 1) & (me[1] == 0) & (me[2] == 0)
+    pl.when(jnp.logical_not(after_filter))(spread_gas)
 
     def filter_one(k, carry):
         below, above = ry_v[0, pl.ds(7 * k, 6)], ry_v[1, pl.ds(7 * k, 6)]
@@ -380,6 +386,8 @@
         for n, s in enumerate((-1, 1)):
             send([((s, 0, 0), part(n, sx_v, 4, g), part(1 - n, rx_v, 4, g), x_ss.at[n], x_rs.at[1 - n])])
             send([((2 * s, 0, 0), part(n, sx2_v, 1, g), part(1 - n, rx2_v, 1, g), x2_ss.at[n], x2_rs.at[1 - n])])
+
+    pl.when(after_filter)(spread_gas)
 
     for n in range(2):
         wait_recv((0, (-1, 1)[n], 0), ry_v.at[n, pl.ds(35, 3)], y_rs.at[n, 3])

time: 23.6 us -> 23 us (0.975)
  the two profiles are of different devices: /device:TPU:8 before, /device:TPU:2 now
where the time goes in v4:
time: 23 us; the launch traced here: 22.8 us
  Pallas kernels  22.2 us (97%)
  between operations  0.64 us (3%)
    pallas_call x1, Pallas kernels, shards(): pl.pallas_call(functools.partial(kernel, sizes), out_shape=out_shape, in_...  21.5 us
    pallas_call x1, Pallas kernels, shards(): pl.pallas_call(store, out_shape=out_shape, in_specs=[any_space] * 2, out_...  0.72 us

profile of v4, /device:TPU:2, one launch (start us, length us, event | category | flops | bytes accessed | tf_op | source)
XLA Modules:
  0.0 22.8 jit_solution(3185765345466188368)
XLA Ops:
  0.6 21.5 %deposit_filter_drag.1 = (f32[5,4,8,128]{3,2,1,0:T(8,128)S(1)}, f32[3,4,4,8,128]{4,3,2,1,0:T(8,128)S(1)}) custom-call(s32[4,8,128]{2,1,0:T(8,128)} %counts_h.1, f32[3,4,4,8,128]{4,3,2,1,0:T(8,128)} %offsets_h.1, f32[4,4,8,128]{3,2,1,0:T(8,128)} %volume_h.1, f32[4,4,8,128]{3,2,1,0:T(8,128)} %beta_h.1, f32[3,4,4,8,128]{4,3,2,1,0:T(8,128)} %pv_h.1, ...), custom_call_target="tpu_custom_call" | custom-call | tf_op jit(solution)/shard_map/deposit_filter_drag/pallas_call | solution.py:470
  22.1 0.7 %store.1 = (f32[5,4,8,128]{3,2,1,0:T(8,128)}, f32[3,4,4,8,128]{4,3,2,1,0:T(8,128)}) custom-call(f32[5,4,8,128]{3,2,1,0:T(8,128)S(1)} %get-tuple-element.4.filtered_v, f32[3,4,4,8,128]{4,3,2,1,0:T(8,128)S(1)} %get-tuple-element.5.drag_v), custom_call_target="tpu_custom_call" | custom-call | tf_op jit(solution)/shard_map/store/pallas_call | solution.py:488

commit v5 on v4

--- a/solution.py
+++ b/solution.py
@@ -17,7 +17,7 @@
 ITERS = 4
 FILTER = 2.0
 
-GROUPS = ((0, 2), (2, 4), (4, 5))
+SIDES = ((1, 0), (0, 1), (1, 1))
 DIAG = ((-1, -1), (-1, 1), (1, -1), (1, 1))
 ALL = ([(0, a, b) for a in (-1, 0, 1) for b in (-1, 0, 1) if (a, b) != (0, 0)]
        + [(-1, 0, 0), (1, 0, 0), (-2, 0, 0), (2, 0, 0)])
@@ -43,8 +43,8 @@
 
 def kernel(sizes, counts_h, offsets_h, volume_h, beta_h, pv_h, gas_h, filtered_o, drag_o,
            counts_v, offsets_v, src_v, pv_v, gas_v, occ_v, prod_v, shifted_v, dm_v, dy_v, dz_v, dyz_v,
-           sy_v, sz_v, sd_v, sx_v, sx2_v, ry_v, rz_v, rd_v, rx_v, rx2_v, sgz_v,
-           in_sem, y_ss, z_ss, d_ss, x_ss, x2_ss, y_rs, z_rs, d_rs, gx_rs, x_rs, x2_rs, late_sem):
+           sy_v, sz_v, sd_v, sx_v, sx2_v, ry_v, rz_v, rd_v, rx_v, rx2_v, sgz_v, by_v, bz_v, bd_v, rg_v,
+           in_sem, y_ss, z_ss, d_ss, x_ss, x2_ss, y_rs, z_rs, d_rs, gx_rs, x_rs, x2_rs, late_sem, b_rs, pg_ss, pg_rs):
     me = (lax.axis_index("gx"), lax.axis_index("gy"), lax.axis_index("gz"))
 
     def near(step):
@@ -85,9 +85,13 @@
         def _():
             copy(step, src, src, ssem, ssem).wait_send()
 
-    is_origin = (me[0] == 0) & (me[1] == 0) & (me[2] == 0)
+    def at(*place):
+        return (me[0] == place[0]) & (me[1] == place[1]) & (me[2] == place[2])
+
+    is_origin, is_proxy = at(0, 0, 0), at(1, 0, 0)
+    is_beside = at(0, 1, 0) | at(0, 0, 1) | at(0, 1, 1)
     barrier = pltpu.get_barrier_semaphore()
-    late = [step for step in ALL if min(step) >= 0 and all(s < n for s, n in zip(step, sizes))]
+    late = [step for step in ALL if min(step) >= 0]
 
     @pl.when(is_origin)
     def _():
@@ -111,6 +115,16 @@
         _, ok, origin = near(step)
         greets = ok if origin is None else ok & jnp.logical_not(origin)
         greeted = greeted + greets.astype(jnp.int32)
+    greeted = greeted + 3 * is_proxy.astype(jnp.int32) + is_beside.astype(jnp.int32)
+
+    @pl.when(is_beside)
+    def _():
+        pl.semaphore_signal(barrier, inc=1, device_id=(1, 0, 0), device_id_type=MESH)
+
+    @pl.when(is_proxy)
+    def _():
+        for a, b in SIDES:
+            pl.semaphore_signal(barrier, inc=1, device_id=(0, a, b), device_id_type=MESH)
 
     @pl.when(jnp.logical_not(is_origin))
     def _():
@@ -135,6 +149,15 @@
     for n, (a, b) in enumerate(DIAG):
         clear((0, a, b), [rd_v.at[n]])
 
+    def fill(which, refs):
+        @pl.when(which)
+        def _():
+            for ref in refs:
+                ref[...] = jnp.zeros(ref.shape, F32)
+
+    fill(is_origin, [ry_v.at[1, pl.ds(0, 35)], rz_v.at[1, pl.ds(0, 10)], rd_v.at[3, pl.ds(0, 5)],
+                     gas_v.at[:, 0], gas_v.at[:, 5]])
+
     row = lax.broadcasted_iota(jnp.int32, (8, 128), 0)
     lane = lax.broadcasted_iota(jnp.int32, (8, 128), 1)
     slot, col = lane >> 3, lane & 7
@@ -158,8 +181,7 @@
         return jnp.where(edge_cols, -image, spill)
 
     def part(n, ref, per, g):
-        first, last = GROUPS[g]
-        return ref.at[n, pl.ds(per * first, per * (last - first))]
+        return ref.at[n, pl.ds(2 * per * g, per if isinstance(g, int) and g == 2 else 2 * per)]
 
     def gas_x(n):
         return ((-1, 1)[n], 0, 0), sx_v.at[n, pl.ds(20, 3)], rx_v.at[1 - n, pl.ds(20, 3)], x_ss.at[n], gx_rs.at[1 - n]
@@ -178,11 +200,38 @@
                  to_origin)
 
     def wait_group(g):
+        @pl.when(jnp.logical_not(is_origin))
+        def _():
+            for n in range(2):
+                wait_recv((0, (-1, 1)[n], 0), part(n, ry_v, 7, g), y_rs.at[n, g])
+                wait_recv((0, 0, (-1, 1)[n]), part(n, rz_v, 2, g), z_rs.at[n, g])
+            for n, (a, b) in enumerate(DIAG):
+                wait_recv((0, a, b), part(n, rd_v, 1, g), d_rs.at[n, g])
+
+    def take_gas(n):
+        wait_recv(((-1, 1)[n], 0, 0), rx_v.at[n, pl.ds(20, 3)], gx_rs.at[n])
+        for j in range(3):
+            gas_v[j, 5 * n] = rx_v[n, 20 + j]
+
+    def pack(planes, first):
+        result = jnp.zeros((8, 128), F32)
+        for i in range(planes.shape[0]):
+            result = jnp.where(slot == first + i, rot(planes[i], 8 * (first + i) + 4, 1), result)
+        return result
+
+    def spread_gas():
+        for j in range(3):
+            sgz_v[j] = pack(gas_v[j], 4)
+            for i in range(6):
+                sy_v[0, 35 + j, pl.ds(i, 1), :] = gas_v[j, i, pl.ds(0, 1), :]
+                sy_v[1, 35 + j, pl.ds(i, 1), :] = gas_v[j, i, pl.ds(7, 1), :]
+            for n in range(2):
+                sy_v[n, 35 + j, pl.ds(6, 2), :] = jnp.zeros((2, 128), F32)
         for n in range(2):
-            wait_recv((0, (-1, 1)[n], 0), part(n, ry_v, 7, g), y_rs.at[n, g])
-            wait_recv((0, 0, (-1, 1)[n]), part(n, rz_v, 2, g), z_rs.at[n, g])
+            send([((0, (-1, 1)[n], 0), sy_v.at[n, pl.ds(35, 3)], ry_v.at[1 - n, pl.ds(35, 3)], y_ss.at[n], y_rs.at[1 - n, 3])])
+            send([((0, 0, (-1, 1)[n]), sgz_v, rz_v.at[1 - n, pl.ds(10, 3)], z_ss.at[n], z_rs.at[1 - n, 3])])
         for n, (a, b) in enumerate(DIAG):
-            wait_recv((0, a, b), part(n, rd_v, 1, g), d_rs.at[n, g])
+            send([((0, a, b), sgz_v, rd_v.at[3 - n, pl.ds(5, 3)], d_ss.at[n], d_rs.at[3 - n, 3])])
 
     loads[0].wait()
     loads[1].wait()
@@ -215,17 +264,12 @@
     @pl.when(is_origin)
     def _():
         send_gas_x(None)
+        spread_gas()
 
     for load in loads[3:]:
         load.wait()
     for j in range(3):
         src_v[2 + j] = src_v[1] * pv_v[j]
-
-    def pack(planes, first):
-        result = jnp.zeros((8, 128), F32)
-        for i in range(planes.shape[0]):
-            result = jnp.where(slot == first + i, rot(planes[i], 8 * (first + i) + 4, 1), result)
-        return result
 
     def unpack(tile, first, count):
         return jnp.stack([rot(tile, -(8 * (first + i) + 4), 1) for i in range(count)])
@@ -276,12 +320,22 @@
             sd_v[n, k] = jnp.where(row_low, first[(b + 1) // 2], second[(b + 1) // 2])
         return carry
 
-    for g in range(3):
-        lax.fori_loop(*GROUPS[g], deposit, 0, unroll=True)
+    def deposit_two(g, carry):
+        deposit(2 * g, carry)
+        deposit(2 * g + 1, carry)
 
         @pl.when(is_origin)
         def _():
             send_group(g, None)
+
+        return carry
+
+    lax.fori_loop(0, 2, deposit_two, 0)
+    deposit(4, 0)
+
+    @pl.when(is_origin)
+    def _():
+        send_group(2, None)
 
     @pl.when(jnp.logical_not(is_origin))
     def _():
@@ -290,38 +344,76 @@
         for g in range(3):
             send_group(g, False)
 
+    to_proxy = [(at(0, a, b), copy((1, -a, -b), src, dst, ssem, b_rs.at[n]))
+                for n, ((a, b), src, dst, ssem) in enumerate((
+                    (SIDES[0], sy_v.at[0, pl.ds(0, 35)], by_v, y_ss.at[0]),
+                    (SIDES[1], sz_v.at[0, pl.ds(0, 10)], bz_v, z_ss.at[0]),
+                    (SIDES[2], sd_v.at[0, pl.ds(0, 5)], bd_v, d_ss.at[0])))]
+    for here, item in to_proxy:
+        pl.when(here)(item.start)
+
+    @pl.when(is_proxy)
+    def _():
+        for a, b in SIDES:
+            copy((-1, a, b), sx_v.at[0, pl.ds(20, 3)], rg_v, pg_ss, pg_rs).start()
+
     by_origin = jnp.bool_(False)
     for step in ALL:
         if max(step) <= 0:
             by_origin = by_origin | near(step)[2]
 
-    @pl.when(by_origin)
+    @pl.when(by_origin & jnp.logical_not(is_proxy))
     def _():
         pl.semaphore_wait(late_sem, 1)
-        send_gas_x(True)
-        for g in range(3):
-            send_group(g, True)
-
-    def spread_gas():
-        for n in range(2):
-            wait_recv(((-1, 1)[n], 0, 0), rx_v.at[n, pl.ds(20, 3)], gx_rs.at[n])
-        for j in range(3):
-            gas_v[j, 0] = rx_v[0, 20 + j]
-            gas_v[j, 5] = rx_v[1, 20 + j]
-            sgz_v[j] = pack(gas_v[j], 4)
-            for i in range(6):
-                sy_v[0, 35 + j, pl.ds(i, 1), :] = gas_v[j, i, pl.ds(0, 1), :]
-                sy_v[1, 35 + j, pl.ds(i, 1), :] = gas_v[j, i, pl.ds(7, 1), :]
-            for n in range(2):
-                sy_v[n, 35 + j, pl.ds(6, 2), :] = jnp.zeros((2, 128), F32)
-        for n in range(2):
-            send([((0, (-1, 1)[n], 0), sy_v.at[n, pl.ds(35, 3)], ry_v.at[1 - n, pl.ds(35, 3)], y_ss.at[n], y_rs.at[1 - n, 3])])
-            send([((0, 0, (-1, 1)[n]), sgz_v, rz_v.at[1 - n, pl.ds(10, 3)], z_ss.at[n], z_rs.at[1 - n, 3])])
-        for n, (a, b) in enumerate(DIAG):
-            send([((0, a, b), sgz_v, rd_v.at[3 - n, pl.ds(5, 3)], d_ss.at[n], d_rs.at[3 - n, 3])])
-
-    after_filter = (me[0] == 1) & (me[1] == 0) & (me[2] == 0)
-    pl.when(jnp.logical_not(after_filter))(spread_gas)
+
+    @pl.when(jnp.logical_not(is_origin | is_proxy))
+    def _():
+        take_gas(0)
+        take_gas(1)
+        spread_gas()
+
+
+    def convolve(m, y, z, yz):
+        edge_m, edge_y = unpack(z, 4, 6), unpack(yz, 4, 6)
+        parts = [None] * 5
+
+        def add(sum_s, sum_c, value):
+            for d in range(5 - sum_s - sum_c):
+                term = value * F32(TAPS[d, sum_s, sum_c])
+                parts[d] = term if parts[d] is None else parts[d] + term
+
+        for c in range(5):
+            rows = []
+            for kind, (tiles, edge) in enumerate(((m, edge_m), (y, edge_y))):
+                if c and not (kind and c == 4):
+                    tiles = (rot(jnp.where(lane < c, edge, tiles), -c, 2)
+                             + rot(jnp.where(lane >= 128 - c, edge, tiles), c, 2))
+                rows.append(tiles)
+            add(0, c, rows[0])
+            for s in range(1, 5 - c):
+                add(s, c, rot(jnp.where(row < s, rows[1], rows[0]), -s, 1)
+                    + rot(jnp.where(row >= 8 - s, rows[1], rows[0]), s, 1))
+        pushed = [None] * 14
+        for i in range(6):
+            for d in range(5):
+                for q in {i + 4 - d, i + 4 + d}:
+                    pushed[q] = parts[d][i] if pushed[q] is None else pushed[q] + parts[d][i]
+        return pushed
+
+    row_in, col_in = ~row_low, ~col_low
+    ends = (lane0 | lane127)[None]
+
+    def around(k):
+        tiles, halo, diag = by_v[pl.ds(7 * k, 6)], by_v[7 * k + 6], bd_v[k]
+        low_m = bz_v[2 * k] + jnp.where(row_in, diag, 0.0)
+        low_y = bz_v[2 * k + 1] + jnp.where(row_in, 0.0, diag)
+        m = jnp.where(row_in[None], tiles, 0.0) + jnp.where(ends, unpack(jnp.where(col_in, 0.0, low_m), 4, 6), 0.0)
+        y = jnp.where(row_in[None], 0.0, tiles) + jnp.where(ends, unpack(jnp.where(col_in, 0.0, low_y), 4, 6), 0.0)
+        z = jnp.where(row_in, halo, 0.0) + jnp.where(col_in, low_m, 0.0)
+        yz = jnp.where(row_in, 0.0, halo) + jnp.where(col_in, low_y, 0.0)
+        pushed = convolve(m, y, z, yz)
+        own = [pushed[5 + i] - pushed[3 - i] for i in range(3)] + [pushed[8]]
+        return own, pushed[9:13], pushed[13]
 
     def filter_one(k, carry):
         below, above = ry_v[0, pl.ds(7 * k, 6)], ry_v[1, pl.ds(7 * k, 6)]
@@ -335,33 +427,9 @@
                          rz_v[n, 2 * k + 1] + jnp.where(row_low, upper, lower)))
         z = dz_v[k] + jnp.where(col_low, side[0][0], side[1][0]) + jnp.where(row_low, below_z, above_z)
         yz = dyz_v[k] + jnp.where(col_low, side[0][1], side[1][1]) + jnp.where(row_low, above_z, below_z)
-        ends = (lane0 | lane127)[None]
         m = m + jnp.where(ends, unpack(jnp.where(col_low, side[1][0], side[0][0]), 4, 6), 0.0)
         y = y + jnp.where(ends, unpack(jnp.where(col_low, side[1][1], side[0][1]), 4, 6), 0.0)
-        edge_m, edge_y = unpack(z, 4, 6), unpack(yz, 4, 6)
-        pushed = [None] * 14
-        for i in range(6):
-            parts = [None] * 5
-
-            def add(sum_s, sum_c, value):
-                for d in range(5 - sum_s - sum_c):
-                    term = value * F32(TAPS[d, sum_s, sum_c])
-                    parts[d] = term if parts[d] is None else parts[d] + term
-
-            for c in range(5):
-                rows = []
-                for kind, (tile, edge) in enumerate(((m[i], edge_m[i]), (y[i], edge_y[i]))):
-                    if c and not (kind and c == 4):
-                        tile = (rot(jnp.where(lane < c, edge, tile), -c, 1)
-                                + rot(jnp.where(lane >= 128 - c, edge, tile), c, 1))
-                    rows.append(tile)
-                add(0, c, rows[0])
-                for s in range(1, 5 - c):
-                    add(s, c, rot(jnp.where(row < s, rows[1], rows[0]), -s, 0)
-                        + rot(jnp.where(row >= 8 - s, rows[1], rows[0]), s, 0))
-            for d in range(5):
-                for q in {i + 4 - d, i + 4 + d}:
-                    pushed[q] = parts[d] if pushed[q] is None else pushed[q] + parts[d]
+        pushed = convolve(m, y, z, yz)
         for i in range(4):
             sx_v[0, 4 * k + i] = pushed[1 + i]
             filtered_o[k, i] = pushed[5 + i]
@@ -380,20 +448,96 @@
                 rx_v[1, 4 * k + i] = -pushed[13 - i]
         return carry
 
-    for g in range(3):
+    def push(first, count, to_origin=None):
+        for n, s in enumerate((-1, 1)):
+            tiles = pl.ds(4 * first, 4 * count)
+            send([((s, 0, 0), sx_v.at[n, tiles], rx_v.at[1 - n, tiles], x_ss.at[n], x_rs.at[1 - n])], to_origin)
+
+    def push_far(to_origin=None):
+        for n, s in enumerate((-1, 1)):
+            send([((2 * s, 0, 0), sx2_v.at[n], rx2_v.at[1 - n], x2_ss.at[n], x2_rs.at[1 - n])], to_origin)
+
+    def filter_and_push(k, carry):
+        filter_one(k, carry)
+
+        @pl.when(jnp.logical_not(is_proxy))
+        def _():
+            push(k, 1)
+
+        return carry
+
+    def filter_two(g, carry):
         wait_group(g)
-        lax.fori_loop(*GROUPS[g], filter_one, 0, unroll=True)
-        for n, s in enumerate((-1, 1)):
-            send([((s, 0, 0), part(n, sx_v, 4, g), part(1 - n, rx_v, 4, g), x_ss.at[n], x_rs.at[1 - n])])
-            send([((2 * s, 0, 0), part(n, sx2_v, 1, g), part(1 - n, rx2_v, 1, g), x2_ss.at[n], x2_rs.at[1 - n])])
-
-    pl.when(after_filter)(spread_gas)
+        filter_and_push(2 * g, carry)
+        filter_and_push(2 * g + 1, carry)
+        return carry
+
+    lax.fori_loop(0, 2, filter_two, 0)
+    wait_group(2)
+    filter_and_push(4, 0)
+
+    @pl.when(jnp.logical_not(is_proxy))
+    def _():
+        push_far()
+
+    def around_one(k, carry):
+        @pl.when((k == 0) & is_proxy)
+        def _():
+            for n, dst in enumerate((by_v, bz_v, bd_v)):
+                copy((-1, 0, 0), dst, dst, b_rs.at[n], b_rs.at[n]).wait_recv()
+
+        @pl.when(is_proxy)
+        def _():
+            own, right, far = around(k)
+            for i in range(4):
+                filtered_o[k, i] += right[i]
+                sx_v[0, 4 * k + i] += own[i]
+            sx_v[1, 4 * k] += far
+
+        return carry
+
+    lax.fori_loop(0, 5, around_one, 0)
+
+    @pl.when(is_proxy)
+    def _():
+        push(0, 5, False)
+        push_far(False)
+        pl.semaphore_wait(late_sem, 1)
+        send_gas_x(True)
+        push(0, 5, True)
+        push_far(True)
+
+    @pl.when(is_origin)
+    def _():
+        take_gas(1)
+
+    @pl.when(is_proxy)
+    def _():
+        take_gas(0)
+        take_gas(1)
+        spread_gas()
+
 
     for n in range(2):
         wait_recv((0, (-1, 1)[n], 0), ry_v.at[n, pl.ds(35, 3)], y_rs.at[n, 3])
         wait_recv((0, 0, (-1, 1)[n]), rz_v.at[n, pl.ds(10, 3)], z_rs.at[n, 3])
     for n, (a, b) in enumerate(DIAG):
         wait_recv((0, a, b), rd_v.at[n, pl.ds(5, 3)], d_rs.at[n, 3])
+
+    @pl.when(is_beside)
+    def _():
+        copy((1, 0, 0), rg_v, rg_v, pg_rs, pg_rs).wait_recv()
+
+    @pl.when(at(0, 1, 0))
+    def _():
+        for j in range(3):
+            ry_v[0, 35 + j, pl.ds(5, 1), :] = rg_v[j, pl.ds(7, 1), :]
+
+    for y, ref, tile in ((0, rz_v, 10), (1, rd_v, 5)):
+        @pl.when(at(0, y, 1))
+        def _():
+            for j in range(3):
+                ref[0, tile + j] = jnp.where(slot == 9, rot(rg_v[j], 76, 1), ref[0, tile + j])
 
     def shift(j, carry):
         tiles = gas_v[j]
@@ -441,12 +585,19 @@
             filtered_o[k, i] = total
 
     for n, s in enumerate((-1, 1)):
+        wait_send((s, 0, 0), sx_v.at[n], x_ss.at[n])
+        wait_send((2 * s, 0, 0), sx2_v.at[n], x2_ss.at[n])
+
+    for n, s in enumerate((-1, 1)):
         wait_send((0, s, 0), sy_v.at[n], y_ss.at[n])
         wait_send((0, 0, s), sz_v.at[n], z_ss.at[n])
-        wait_send((s, 0, 0), sx_v.at[n], x_ss.at[n])
-        wait_send((2 * s, 0, 0), sx2_v.at[n], x2_ss.at[n])
     for n, (a, b) in enumerate(DIAG):
         wait_send((0, a, b), sd_v.at[n], d_ss.at[n])
+
+    @pl.when(is_proxy)
+    def _():
+        nine = sx_v.at[0, pl.ds(0, 9)]
+        copy((1, 0, 0), nine, nine, pg_ss, pg_ss).wait_send()
 
 
 def store(filtered_v, drag_v, filtered_h, drag_h, sem):
@@ -477,8 +628,10 @@
                 vmem(4, 4), vmem(27, 4, 4), vmem(3, 9, 6), vmem(5, 6), vmem(5, 6), vmem(5), vmem(5),
                 vmem(2, 38), vmem(2, 13), vmem(4, 8), vmem(2, 23), vmem(2, 5),
                 vmem(2, 38), vmem(2, 13), vmem(4, 8), vmem(2, 23), vmem(2, 5), vmem(3),
+                vmem(35), vmem(10), vmem(5), vmem(3),
                 dma((6,)), dma((2,)), dma((2,)), dma((4,)), dma((2,)), dma((2,)),
                 dma((2, 4)), dma((2, 4)), dma((4, 4)), dma((2,)), dma((2,)), dma((2,)), pltpu.SemaphoreType.REGULAR,
+                dma((3,)), dma, dma,
             ],
             compiler_params=pltpu.CompilerParams(
                 collective_id=0, has_side_effects=True, vmem_limit_bytes=32 * 2**20),

time: 23 us -> 22.5 us (0.978)
  the two profiles are of different devices: /device:TPU:2 before, /device:TPU:66 now
where the time goes in v5:
time: 22.5 us; the launch traced here: 22.3 us
  Pallas kernels  21.7 us (96%)
  between operations  0.64 us (3%)
    pallas_call x1, Pallas kernels, shards(): pl.pallas_call(functools.partial(kernel, sizes), out_shape=out_shape, in_...  21 us
    pallas_call x1, Pallas kernels, shards(): pl.pallas_call(store, out_shape=out_shape, in_specs=[any_space] * 2, out_...  0.72 us

profile of v5, /device:TPU:66, one launch (start us, length us, event | category | flops | bytes accessed | tf_op | source)
XLA Modules:
  0.0 22.3 jit_solution(2862558623624670556)
XLA Ops:
  0.6 21.0 %deposit_filter_drag.1 = (f32[5,4,8,128]{3,2,1,0:T(8,128)S(1)}, f32[3,4,4,8,128]{4,3,2,1,0:T(8,128)S(1)}) custom-call(s32[4,8,128]{2,1,0:T(8,128)} %counts_h.1, f32[3,4,4,8,128]{4,3,2,1,0:T(8,128)} %offsets_h.1, f32[4,4,8,128]{3,2,1,0:T(8,128)} %volume_h.1, f32[4,4,8,128]{3,2,1,0:T(8,128)} %beta_h.1, f32[3,4,4,8,128]{4,3,2,1,0:T(8,128)} %pv_h.1, ...), custom_call_target="tpu_custom_call" | custom-call | tf_op jit(solution)/shard_map/deposit_filter_drag/pallas_call | solution.py:621
  21.6 0.7 %store.1 = (f32[5,4,8,128]{3,2,1,0:T(8,128)}, f32[3,4,4,8,128]{4,3,2,1,0:T(8,128)}) custom-call(f32[5,4,8,128]{3,2,1,0:T(8,128)S(1)} %get-tuple-element.4.filtered_v, f32[3,4,4,8,128]{4,3,2,1,0:T(8,128)S(1)} %get-tuple-element.5.drag_v), custom_call_target="tpu_custom_call" | custom-call | tf_op jit(solution)/shard_map/store/pallas_call | solution.py:641

commit v6 on v5

--- a/solution.py
+++ b/solution.py
@@ -44,7 +44,7 @@
 def kernel(sizes, counts_h, offsets_h, volume_h, beta_h, pv_h, gas_h, filtered_o, drag_o,
            counts_v, offsets_v, src_v, pv_v, gas_v, occ_v, prod_v, shifted_v, dm_v, dy_v, dz_v, dyz_v,
            sy_v, sz_v, sd_v, sx_v, sx2_v, ry_v, rz_v, rd_v, rx_v, rx2_v, sgz_v, by_v, bz_v, bd_v, rg_v,
-           in_sem, y_ss, z_ss, d_ss, x_ss, x2_ss, y_rs, z_rs, d_rs, gx_rs, x_rs, x2_rs, late_sem, b_rs, pg_ss, pg_rs):
+           in_sem, y_ss, z_ss, d_ss, x_ss, x2_ss, y_rs, z_rs, d_rs, gx_rs, x_rs, x2_rs, late_sem, b_rs, o_ss, pg_ss, pg_rs):
     me = (lax.axis_index("gx"), lax.axis_index("gy"), lax.axis_index("gz"))
 
     def near(step):
@@ -89,13 +89,14 @@
         return (me[0] == place[0]) & (me[1] == place[1]) & (me[2] == place[2])
 
     is_origin, is_proxy = at(0, 0, 0), at(1, 0, 0)
-    is_beside = at(0, 1, 0) | at(0, 0, 1) | at(0, 1, 1)
+    is_late = [(me[0] == x) & (me[1] <= 1) & (me[2] == 1) for x in range(3)]
+    is_beside = [is_late[x] | at(x, 1, 0) for x in range(2)]
     barrier = pltpu.get_barrier_semaphore()
     late = [step for step in ALL if min(step) >= 0]
 
     @pl.when(is_origin)
     def _():
-        pl.semaphore_wait(barrier, len(late))
+        pl.semaphore_wait(barrier, len(late) + 5)
         for step in late:
             pl.semaphore_signal(late_sem, inc=1, device_id=step, device_id_type=MESH)
 
@@ -115,9 +116,13 @@
         _, ok, origin = near(step)
         greets = ok if origin is None else ok & jnp.logical_not(origin)
         greeted = greeted + greets.astype(jnp.int32)
-    greeted = greeted + 3 * is_proxy.astype(jnp.int32) + is_beside.astype(jnp.int32)
-
-    @pl.when(is_beside)
+    greeted = greeted + 3 * is_proxy.astype(jnp.int32) + is_beside[0].astype(jnp.int32)
+
+    @pl.when(is_beside[1] | is_late[2])
+    def _():
+        pl.semaphore_signal(barrier, inc=1, device_id=(0, 0, 0), device_id_type=MESH)
+
+    @pl.when(is_beside[0])
     def _():
         pl.semaphore_signal(barrier, inc=1, device_id=(1, 0, 0), device_id_type=MESH)
 
@@ -157,6 +162,12 @@
 
     fill(is_origin, [ry_v.at[1, pl.ds(0, 35)], rz_v.at[1, pl.ds(0, 10)], rd_v.at[3, pl.ds(0, 5)],
                      gas_v.at[:, 0], gas_v.at[:, 5]])
+    fill(is_proxy, [gas_v.at[:, 0]])
+    fill(at(0, 0, 1), [rz_v.at[0, pl.ds(0, 10)]])
+    fill(at(0, 1, 1), [rd_v.at[0, pl.ds(0, 5)]])
+    fill(is_late[0] | is_late[1], [by_v])
+    fill((is_late[0] | is_late[1] | is_late[2]) & (me[1] == 0), [bd_v])
+    fill((is_late[0] | is_late[1] | is_late[2]) & (me[1] == 1), [bz_v])
 
     row = lax.broadcasted_iota(jnp.int32, (8, 128), 0)
     lane = lax.broadcasted_iota(jnp.int32, (8, 128), 1)
@@ -190,23 +201,52 @@
         for n in range(2):
             send([gas_x(n)], to_origin)
 
-    def send_group(g, to_origin):
+    def send_y(g):
+        for n in range(2):
+            send([((0, (-1, 1)[n], 0), part(n, sy_v, 7, g), part(1 - n, ry_v, 7, g), y_ss.at[n], y_rs.at[1 - n, g])], False)
+
+    def send_zd():
         for n, (a, b) in enumerate(DIAG):
-            send([((0, a, b), part(n, sd_v, 1, g), part(3 - n, rd_v, 1, g), d_ss.at[n], d_rs.at[3 - n, g])], to_origin)
+            send([((0, a, b), sd_v.at[n, pl.ds(0, 5)], rd_v.at[3 - n, pl.ds(0, 5)], d_ss.at[n], d_rs.at[3 - n, 0])], False)
         for n in range(2):
-            send([((0, 0, (-1, 1)[n]), part(n, sz_v, 2, g), part(1 - n, rz_v, 2, g), z_ss.at[n], z_rs.at[1 - n, g])],
-                 to_origin)
-            send([((0, (-1, 1)[n], 0), part(n, sy_v, 7, g), part(1 - n, ry_v, 7, g), y_ss.at[n], y_rs.at[1 - n, g])],
-                 to_origin)
-
-    def wait_group(g):
+            send([((0, 0, (-1, 1)[n]), sz_v.at[n, pl.ds(0, 10)], rz_v.at[1 - n, pl.ds(0, 10)], z_ss.at[n],
+                   z_rs.at[1 - n, 0])], False)
+
+    def wait_part(step, dst, rsem):
+        _, ok, origin = near(step)
+
+        @pl.when(ok if origin is None else ok & jnp.logical_not(origin))
+        def _():
+            copy(step, dst, dst, rsem, rsem).wait_recv()
+
+    def wait_y(g):
+        for n in range(2):
+            @pl.when(jnp.logical_not(is_origin))
+            def _():
+                wait_recv((0, (-1, 1)[n], 0), part(n, ry_v, 7, g), y_rs.at[n, g])
+
+    def wait_zd():
         @pl.when(jnp.logical_not(is_origin))
         def _():
             for n in range(2):
-                wait_recv((0, (-1, 1)[n], 0), part(n, ry_v, 7, g), y_rs.at[n, g])
-                wait_recv((0, 0, (-1, 1)[n]), part(n, rz_v, 2, g), z_rs.at[n, g])
+                wait_part((0, 0, (-1, 1)[n]), rz_v.at[n, pl.ds(0, 10)], z_rs.at[n, 0])
             for n, (a, b) in enumerate(DIAG):
-                wait_recv((0, a, b), part(n, rd_v, 1, g), d_rs.at[n, g])
+                wait_part((0, a, b), rd_v.at[n, pl.ds(0, 5)], d_rs.at[n, 0])
+
+    AROUND = ((2, sz_v, 1, bz_v), (1, sd_v, 3, bd_v))
+
+    def send_around(g):
+        first, last = ((0, 4), (4, 5))[g]
+        for n, ((a, b), (per, src, at_n, dst)) in enumerate(zip(SIDES[1:], AROUND)):
+            tiles = pl.ds(per * first, per * (last - first))
+            for x in range(2):
+                copy((x, a, b), src.at[at_n, tiles], dst.at[tiles], o_ss.at[n], b_rs.at[g]).start()
+            if g:
+                tiles = pl.ds(0, 5 * per)
+                copy((2, a, b), src.at[at_n, tiles], dst.at[tiles], o_ss.at[n], b_rs.at[0]).start()
+
+    def origin_y(g):
+        return (0, 1, 0), part(1, sy_v, 7, g), part(0, ry_v, 7, g), y_ss.at[1], y_rs.at[0, g]
 
     def take_gas(n):
         wait_recv(((-1, 1)[n], 0, 0), rx_v.at[n, pl.ds(20, 3)], gx_rs.at[n])
@@ -229,9 +269,9 @@
                 sy_v[n, 35 + j, pl.ds(6, 2), :] = jnp.zeros((2, 128), F32)
         for n in range(2):
             send([((0, (-1, 1)[n], 0), sy_v.at[n, pl.ds(35, 3)], ry_v.at[1 - n, pl.ds(35, 3)], y_ss.at[n], y_rs.at[1 - n, 3])])
-            send([((0, 0, (-1, 1)[n]), sgz_v, rz_v.at[1 - n, pl.ds(10, 3)], z_ss.at[n], z_rs.at[1 - n, 3])])
+            send([((0, 0, (-1, 1)[n]), sgz_v, rz_v.at[1 - n, pl.ds(10, 3)], z_ss.at[n], z_rs.at[1 - n, 1])])
         for n, (a, b) in enumerate(DIAG):
-            send([((0, a, b), sgz_v, rd_v.at[3 - n, pl.ds(5, 3)], d_ss.at[n], d_rs.at[3 - n, 3])])
+            send([((0, a, b), sgz_v, rd_v.at[3 - n, pl.ds(5, 3)], d_ss.at[n], d_rs.at[3 - n, 1])])
 
     loads[0].wait()
     loads[1].wait()
@@ -264,6 +304,8 @@
     @pl.when(is_origin)
     def _():
         send_gas_x(None)
+        for a, b in SIDES:
+            copy((1, a, b), sx_v.at[1, pl.ds(20, 3)], rg_v, pg_ss, pg_rs).start()
         spread_gas()
 
     for load in loads[3:]:
@@ -326,7 +368,11 @@
 
         @pl.when(is_origin)
         def _():
-            send_group(g, None)
+            copy(*origin_y(g)).start()
+
+            @pl.when(g == 1)
+            def _():
+                send_around(0)
 
         return carry
 
@@ -335,14 +381,16 @@
 
     @pl.when(is_origin)
     def _():
-        send_group(2, None)
+        send_around(1)
+        copy(*origin_y(2)).start()
 
     @pl.when(jnp.logical_not(is_origin))
     def _():
         pl.semaphore_wait(barrier, greeted)
         send_gas_x(False)
+        send_zd()
         for g in range(3):
-            send_group(g, False)
+            send_y(g)
 
     to_proxy = [(at(0, a, b), copy((1, -a, -b), src, dst, ssem, b_rs.at[n]))
                 for n, ((a, b), src, dst, ssem) in enumerate((
@@ -366,9 +414,12 @@
     def _():
         pl.semaphore_wait(late_sem, 1)
 
-    @pl.when(jnp.logical_not(is_origin | is_proxy))
-    def _():
-        take_gas(0)
+    @pl.when(jnp.logical_not(is_origin))
+    def _():
+        @pl.when(jnp.logical_not(is_proxy))
+        def _():
+            take_gas(0)
+
         take_gas(1)
         spread_gas()
 
@@ -400,7 +451,10 @@
                     pushed[q] = parts[d][i] if pushed[q] is None else pushed[q] + parts[d][i]
         return pushed
 
-    row_in, col_in = ~row_low, ~col_low
+    turn = is_proxy.astype(jnp.int32)
+    row_in = row + turn * (7 - 2 * row) < 4
+    col_in = col + turn * (7 - 2 * col) < 4
+    first_x = (me[0] == 0).astype(F32)
     ends = (lane0 | lane127)[None]
 
     def around(k):
@@ -467,13 +521,14 @@
         return carry
 
     def filter_two(g, carry):
-        wait_group(g)
+        wait_y(g)
         filter_and_push(2 * g, carry)
         filter_and_push(2 * g + 1, carry)
         return carry
 
+    wait_zd()
     lax.fori_loop(0, 2, filter_two, 0)
-    wait_group(2)
+    wait_y(2)
     filter_and_push(4, 0)
 
     @pl.when(jnp.logical_not(is_proxy))
@@ -481,18 +536,31 @@
         push_far()
 
     def around_one(k, carry):
+        for g in range(2):
+            first, last = ((0, 4), (4, 5))[g]
+            for a, (per, _, _, dst) in enumerate(AROUND):
+                part_in = dst.at[pl.ds(per * first, per * (last - first))]
+
+                @pl.when((k == first) & (is_late[0] | is_late[1]) & (me[1] == a))
+                def _():
+                    copy((0, 0, -1), part_in, part_in, b_rs.at[g], b_rs.at[g]).wait_recv()
+
         @pl.when((k == 0) & is_proxy)
         def _():
             for n, dst in enumerate((by_v, bz_v, bd_v)):
                 copy((-1, 0, 0), dst, dst, b_rs.at[n], b_rs.at[n]).wait_recv()
 
-        @pl.when(is_proxy)
+        @pl.when(is_proxy | is_late[0] | is_late[1])
         def _():
             own, right, far = around(k)
             for i in range(4):
-                filtered_o[k, i] += right[i]
-                sx_v[0, 4 * k + i] += own[i]
-            sx_v[1, 4 * k] += far
+                filtered_o[k, i] += own[i] * first_x + right[i] * (1.0 - first_x)
+
+            @pl.when(is_proxy)
+            def _():
+                for i in range(4):
+                    sx_v[0, 4 * k + i] += own[i]
+                sx_v[1, 4 * k] += far
 
         return carry
 
@@ -514,30 +582,29 @@
     @pl.when(is_proxy)
     def _():
         take_gas(0)
-        take_gas(1)
-        spread_gas()
 
 
     for n in range(2):
         wait_recv((0, (-1, 1)[n], 0), ry_v.at[n, pl.ds(35, 3)], y_rs.at[n, 3])
-        wait_recv((0, 0, (-1, 1)[n]), rz_v.at[n, pl.ds(10, 3)], z_rs.at[n, 3])
+        wait_recv((0, 0, (-1, 1)[n]), rz_v.at[n, pl.ds(10, 3)], z_rs.at[n, 1])
     for n, (a, b) in enumerate(DIAG):
-        wait_recv((0, a, b), rd_v.at[n, pl.ds(5, 3)], d_rs.at[n, 3])
-
-    @pl.when(is_beside)
+        wait_recv((0, a, b), rd_v.at[n, pl.ds(5, 3)], d_rs.at[n, 1])
+
+    @pl.when(is_beside[0] | is_beside[1])
     def _():
         copy((1, 0, 0), rg_v, rg_v, pg_rs, pg_rs).wait_recv()
 
-    @pl.when(at(0, 1, 0))
-    def _():
-        for j in range(3):
-            ry_v[0, 35 + j, pl.ds(5, 1), :] = rg_v[j, pl.ds(7, 1), :]
-
-    for y, ref, tile in ((0, rz_v, 10), (1, rd_v, 5)):
-        @pl.when(at(0, y, 1))
+    for x, i in ((0, 5), (1, 0)):
+        @pl.when(at(x, 1, 0))
         def _():
             for j in range(3):
-                ref[0, tile + j] = jnp.where(slot == 9, rot(rg_v[j], 76, 1), ref[0, tile + j])
+                ry_v[0, 35 + j, pl.ds(i, 1), :] = rg_v[j, pl.ds(7, 1), :]
+
+        for y, ref, tile in ((0, rz_v, 10), (1, rd_v, 5)):
+            @pl.when(at(x, y, 1))
+            def _():
+                for j in range(3):
+                    ref[0, tile + j] = jnp.where(slot == 4 + i, rot(rg_v[j], 8 * i + 36, 1), ref[0, tile + j])
 
     def shift(j, carry):
         tiles = gas_v[j]
@@ -574,6 +641,18 @@
 
     lax.fori_loop(0, 4, drag, 0, unroll=True)
 
+    @pl.when(is_late[2])
+    def _():
+        for a, dst in enumerate((bz_v, bd_v)):
+            @pl.when(me[1] == a)
+            def _():
+                copy((0, 0, -1), dst, dst, b_rs.at[0], b_rs.at[0]).wait_recv()
+
+        for k in range(5):
+            low_m = bz_v[2 * k] + jnp.where(row_in, bd_v[k], 0.0)
+            spill = jnp.where(lane0 | lane127, rot(jnp.where(col_in, 0.0, low_m), -76, 1), 0.0)
+            filtered_o[k, 0] += spill * F32(TAPS[4, 0, 0])
+
     for n, s in enumerate((-1, 1)):
         wait_recv((s, 0, 0), rx_v.at[n, pl.ds(0, 20)], x_rs.at[n])
         wait_recv((2 * s, 0, 0), rx2_v.at[n], x2_rs.at[n])
@@ -588,13 +667,23 @@
         wait_send((s, 0, 0), sx_v.at[n], x_ss.at[n])
         wait_send((2 * s, 0, 0), sx2_v.at[n], x2_ss.at[n])
 
-    for n, s in enumerate((-1, 1)):
-        wait_send((0, s, 0), sy_v.at[n], y_ss.at[n])
-        wait_send((0, 0, s), sz_v.at[n], z_ss.at[n])
-    for n, (a, b) in enumerate(DIAG):
-        wait_send((0, a, b), sd_v.at[n], d_ss.at[n])
-
-    @pl.when(is_proxy)
+    @pl.when(jnp.logical_not(is_origin))
+    def _():
+        for n, s in enumerate((-1, 1)):
+            wait_send((0, s, 0), sy_v.at[n], y_ss.at[n])
+            wait_send((0, 0, s), sz_v.at[n], z_ss.at[n])
+        for n, (a, b) in enumerate(DIAG):
+            wait_send((0, a, b), sd_v.at[n], d_ss.at[n])
+
+    @pl.when(is_origin)
+    def _():
+        wait_send((0, 1, 0), sy_v.at[1], y_ss.at[1])
+        for ssem in (z_ss.at[1], d_ss.at[3]):
+            copy((1, 0, 0), sgz_v, sgz_v, ssem, ssem).wait_send()
+        for n, ref in enumerate((sy_v.at[0, pl.ds(0, 30)], sx_v.at[0, pl.ds(0, 15)])):
+            copy((1, 0, 0), ref, ref, o_ss.at[n], o_ss.at[n]).wait_send()
+
+    @pl.when(is_origin | is_proxy)
     def _():
         nine = sx_v.at[0, pl.ds(0, 9)]
         copy((1, 0, 0), nine, nine, pg_ss, pg_ss).wait_send()
@@ -630,8 +719,8 @@
                 vmem(2, 38), vmem(2, 13), vmem(4, 8), vmem(2, 23), vmem(2, 5), vmem(3),
                 vmem(35), vmem(10), vmem(5), vmem(3),
                 dma((6,)), dma((2,)), dma((2,)), dma((4,)), dma((2,)), dma((2,)),
-                dma((2, 4)), dma((2, 4)), dma((4, 4)), dma((2,)), dma((2,)), dma((2,)), pltpu.SemaphoreType.REGULAR,
-                dma((3,)), dma, dma,
+                dma((2, 4)), dma((2, 2)), dma((4, 2)), dma((2,)), dma((2,)), dma((2,)), pltpu.SemaphoreType.REGULAR,
+                dma((3,)), dma((2,)), dma, dma,
             ],
             compiler_params=pltpu.CompilerParams(
                 collective_id=0, has_side_effects=True, vmem_limit_bytes=32 * 2**20),

time: 22.5 us -> 22.4 us (level)
  the two profiles are of different devices: /device:TPU:66 before, /device:TPU:2 now
where the time goes in v6:
time: 22.4 us; the launch traced here: 22.1 us
  Pallas kernels  21.5 us (96%)
  between operations  0.64 us (3%)
    pallas_call x1, Pallas kernels, shards(): pl.pallas_call(functools.partial(kernel, sizes), out_shape=out_shape, in_...  20.8 us
    pallas_call x1, Pallas kernels, shards(): pl.pallas_call(store, out_shape=out_shape, in_specs=[any_space] * 2, out_...  0.72 us

profile of v6, /device:TPU:2, one launch (start us, length us, event | category | flops | bytes accessed | tf_op | source)
XLA Modules:
  0.0 22.1 jit_solution(9650054366456852980)
XLA Ops:
  0.6 20.8 %deposit_filter_drag.1 = (f32[5,4,8,128]{3,2,1,0:T(8,128)S(1)}, f32[3,4,4,8,128]{4,3,2,1,0:T(8,128)S(1)}) custom-call(s32[4,8,128]{2,1,0:T(8,128)} %counts_h.1, f32[3,4,4,8,128]{4,3,2,1,0:T(8,128)} %offsets_h.1, f32[4,4,8,128]{3,2,1,0:T(8,128)} %volume_h.1, f32[4,4,8,128]{3,2,1,0:T(8,128)} %beta_h.1, f32[3,4,4,8,128]{4,3,2,1,0:T(8,128)} %pv_h.1, ...), custom_call_target="tpu_custom_call" | custom-call | tf_op jit(solution)/shard_map/deposit_filter_drag/pallas_call | solution.py:710
  21.4 0.7 %store.1 = (f32[5,4,8,128]{3,2,1,0:T(8,128)}, f32[3,4,4,8,128]{4,3,2,1,0:T(8,128)}) custom-call(f32[5,4,8,128]{3,2,1,0:T(8,128)S(1)} %get-tuple-element.4.filtered_v, f32[3,4,4,8,128]{4,3,2,1,0:T(8,128)S(1)} %get-tuple-element.5.drag_v), custom_call_target="tpu_custom_call" | custom-call | tf_op jit(solution)/shard_map/store/pallas_call | solution.py:730
